TPU v7x, 32 devices: a whole 2x2x4 slice. The times are simulated.
32 devices in a mesh: parts: 2 (over y), seq: 4 (over z), mp: 2 (over x), rep: 2 (over core).
Axes of the slice: x: 2, y: 2, z: 4, core: 2. Of those that a mesh axis runs over, the one named last changes fastest.
Arguments:
- queries: bfloat16 [6144, 4096], P(('parts', 'seq'), ('mp', 'rep')), parts along dimension 0, may hold values from -110 to 110
- key_weight: bfloat16 [1024, 4096], P(None, ('mp', 'rep')), may hold values from -0.1875 to 0.1875
- value_weight: bfloat16 [1024, 4096], P(None, ('mp', 'rep')), may hold values from -0.1875 to 0.1875
- enc_gain: float32 [1024], P(('mp', 'rep')), may hold values from 0.25 to 1.75
- store: bfloat16 [128, 128, 1024], P(('parts', 'seq'), None, ('mp', 'rep')), parts along dimension 0, may hold values from -330 to 330
- nbr_owner: int32 [96, 2], P(('parts', 'seq')), parts along dimension 0, may hold values from 0 to 3, all different within a row; in each aligned block of 12 rows (0 to 11, 12 to 23, ...) at most 12 rows name the same one
- nbr_slot: int32 [96, 2], P(('parts', 'seq')), parts along dimension 0, may hold values from 0 to 15
- nbr_count: int32 [96], P(('parts', 'seq')), parts along dimension 0, may hold values from 1 to 2
Outputs:
- attended: bfloat16 [6144, 4096], P(('parts', 'seq'), ('mp', 'rep')), parts along dimension 0
There are 2 independent parts, one for each index of `parts`. A program takes and returns all parts, laid end to end along the dimension named above; an argument that names none is the same for every part. Nothing has to cross between parts.
Inputs may be any that keep to these rules, and one draw needn't show every extreme that they name: `nbr_owner`: in each aligned block of 12 stretches no owner is named more than 12 times, and the 2 owners of one stretch differ.
All inputs are finite; a program needn't handle non-finite values.
Results may differ from a plain program's by a relative error of at most 0.0089.
Values may be sent and summed in bfloat16 or wider, within the bound.
No kernel may reach another device: no remote copies, remote signals or barrier semaphores. Data moves between devices by JAX's collectives and lax.ppermute only.
A program may use at most 128 MiB of HBM per device.

v0:
```python
import math

import jax
import jax.numpy as jnp
from jax import lax
from jax.experimental import pallas as pl
from jax.experimental.pallas import tpu as pltpu
from jax.sharding import PartitionSpec as P

HEAD_DIM = 128
DE = 1024
NLEN = 128
STRETCH = 64
KMAX = 2
EPS = 1e-06

SEQ_SPEC = ("parts", "seq")
FEATURES = ("mp", "rep")
VMEM_LIMIT = 28 * 1024 * 1024

CHIPS = 4
ENTRIES_EACH = 16
HALF = 8
ROUNDS = 5
CAP = 4
GROUP = 2
SWEEPS = ROUNDS + 1
SWEPT = (CAP,) * ROUNDS + (2 * CAP,)
LANES = 128

LITTLE = pl.CostEstimate(flops=1, bytes_accessed=1, transcendentals=0)


def shifted(value, axis, steps):
    count = lax.axis_size(axis)
    first, last = max(0, -steps), min(count, count - steps)
    return lax.ppermute(value, axis, [(source, source + steps) for source in range(first, last)])


def swapped(value, axis):
    return lax.ppermute(value, axis, [(0, 1), (1, 0)])


def project(marks, gain, rounds, key_weight, value_weight, group, total, first=0, held=()):
    pieces = len(rounds[0])
    count, tokens, width = rounds[0][0].shape
    columns = key_weight.shape[1]
    each = count // group
    rows = group * tokens
    groups = total // group

    def kernel(marks_ref, gain_ref, *refs):
        arrays, weights = refs[: len(rounds) * pieces], refs[len(rounds) * pieces : len(rounds) * pieces + 2]
        *outs, normed, key_rows, value_rows, sems = refs[-6:]
        step = pl.program_id(0)
        ordered = (key_rows, value_rows)
        copies = [
            pltpu.make_async_copy(
                weight.at[pl.ds(pl.multiple_of(marks_ref[piece] * width, width), width)],
                rows_ref.at[pl.ds(piece * width, width)],
                sems.at[which * pieces + piece],
            )
            for which, (weight, rows_ref) in enumerate(zip(weights, ordered))
            for piece in range(pieces)
        ]

        @pl.when(step == 0)
        def _():
            for copy in copies:
                copy.start()

        wanted = marks_ref[pieces + first + step] > 0
        for number in range(len(rounds)):
            parts = arrays[number * pieces : (number + 1) * pieces]

            @pl.when(wanted & (step >= number * each) & (step < (number + 1) * each))
            def _(number=number, parts=parts):
                at = pl.ds((step - number * each) * group, group)
                raw = [part[at].reshape(rows, width).astype(jnp.float32) for part in parts]
                squares = sum(jnp.sum(part * part, axis=1, keepdims=True) for part in raw)
                scale = lax.rsqrt(squares / DE + EPS)
                for index, part in enumerate(raw):
                    place = slice(index * width, (index + 1) * width)
                    normed[:, place] = (part * scale * gain_ref[:, place]).astype(jnp.bfloat16)

        @pl.when(step == 0)
        def _():
            for copy in copies:
                copy.wait()

        @pl.when(wanted)
        def _():
            states = normed[...]
            for out, weight in zip(outs, ordered):
                product = jnp.dot(states, weight[...], preferred_element_type=jnp.float32)
                out[...] = product.astype(jnp.bfloat16).reshape(out.shape)

    out = jax.ShapeDtypeStruct((total, tokens, columns), jnp.bfloat16)
    out_spec = pl.BlockSpec((group, tokens, columns), lambda i, marks: (jnp.maximum(marks[pieces + groups + first + i], first), 0, 0))
    arrays = [piece for parts in rounds for piece in parts]
    operands = (marks, gain, *arrays, key_weight, value_weight, *held)
    return pl.pallas_call(
        kernel,
        out_shape=(out, out),
        grid_spec=pltpu.PrefetchScalarGridSpec(
            num_scalar_prefetch=1,
            grid=(len(rounds) * each,),
            in_specs=[pl.BlockSpec((1, DE), lambda i, _: (0, 0))]
            + [pl.BlockSpec(memory_space=pltpu.VMEM)] * len(arrays)
            + [pl.BlockSpec(memory_space=pl.ANY)] * (2 + len(held)),
            out_specs=(out_spec, out_spec),
            scratch_shapes=[pltpu.VMEM((rows, DE), jnp.bfloat16)]
            + [pltpu.VMEM((DE, columns), jnp.bfloat16)] * 2
            + [pltpu.SemaphoreType.DMA((2 * pieces,))],
        ),
        input_output_aliases={len(operands) - len(held) + i: i for i in range(len(held))},
        compiler_params=pltpu.CompilerParams(vmem_limit_bytes=47 * 1024 * 1024),
        cost_estimate=LITTLE,
        name="project",
    )(*operands)


SAME_COLUMNS = (((1,), (1,)), ((), ()))
SAME_ROWS = (((0,), (0,)), ((), ()))


def attend_kernel(slots, counts, query_ref, *refs):
    *entries, out_ref = refs
    keys, values = entries[: len(entries) // 2], entries[len(entries) // 2 :]
    together = len(keys) // KMAX
    wide = 2 * HEAD_DIM
    factor = math.log2(math.e) / math.sqrt(HEAD_DIM)
    count = [counts[pl.program_id(0) * together + g] for g in range(together)]
    work = [(g, start) for g in range(together) for start in range(0, query_ref.shape[1], wide)]

    def scored(g, start):
        query = query_ref[g * STRETCH : (g + 1) * STRETCH, start : start + wide]
        left, right = query[:, :HEAD_DIM], query[:, HEAD_DIM:]
        zero = jnp.zeros_like(left)
        both = jnp.concatenate([jnp.concatenate([left, zero], 1), jnp.concatenate([zero, right], 1)], 0)
        one, two = [
            lax.dot_general(
                keys[g * KMAX + k][0, :, start : start + wide], both, SAME_COLUMNS, preferred_element_type=jnp.float32
            )
            for k in range(KMAX)
        ]
        return one, jnp.where(count[g] == 2, two, -1e30)

    def weighed(one, two):
        top = jnp.maximum(one, two).max(0, keepdims=True)
        one, two = jnp.exp2((one - top) * factor), jnp.exp2((two - top) * factor)
        share = 1.0 / (one + two).sum(0, keepdims=True)
        return (one * share).astype(jnp.bfloat16), (two * share).astype(jnp.bfloat16)

    def mix(g, start, weights):
        rows = jnp.concatenate([values[g * KMAX + k][0, :, start : start + wide] for k in range(KMAX)], 0)
        mixed = lax.dot_general(jnp.concatenate(weights, 0), rows, SAME_ROWS, preferred_element_type=jnp.float32)
        mixed = jnp.where(count[g] > 0, mixed, 0.0).astype(jnp.bfloat16)
        rows = slice(g * STRETCH, (g + 1) * STRETCH)
        out_ref[rows, start : start + HEAD_DIM] = mixed[:STRETCH, :HEAD_DIM]
        out_ref[rows, start + HEAD_DIM : start + wide] = mixed[STRETCH:, HEAD_DIM:]

    scores = [scored(*piece) for piece in work]
    weights = [weighed(*pair) for pair in scores]
    for piece, pair in zip(work, weights):
        mix(*piece, pair)


def attend(slots, counts, queries, keys, values, together=3):
    stretches = counts.shape[0]
    columns = queries.shape[1]

    def entry(i):
        return pl.BlockSpec((1, NLEN, columns), lambda step, slots, _: (slots[step * together * KMAX + i], 0, 0))

    query_spec = pl.BlockSpec((together * STRETCH, columns), lambda i, *_: (i, 0))
    entries = [entry(i) for i in range(together * KMAX)]
    return pl.pallas_call(
        attend_kernel,
        out_shape=jax.ShapeDtypeStruct(queries.shape, jnp.bfloat16),
        grid_spec=pltpu.PrefetchScalarGridSpec(
            num_scalar_prefetch=2,
            grid=(stretches // together,),
            in_specs=[query_spec] + entries * 2,
            out_specs=query_spec,
        ),
        compiler_params=pltpu.CompilerParams(vmem_limit_bytes=60 * 1024 * 1024),
        cost_estimate=LITTLE,
        name="attend",
    )(slots, counts, queries, *[keys] * len(entries), *[values] * len(entries))


def plan_kernel(place, table, plan_ref, far_ref, need_ref, lists_ref, picks_ref, slots_ref):
    f32 = jnp.float32
    groups = 2 * CHIPS
    me = place[0]
    each = table.shape[0] // groups
    lane = lax.broadcasted_iota(jnp.int32, (1, LANES), 1)

    bases = [jnp.bitwise_xor(me, group) * each for group in range(groups)]
    need = []
    for group in range(groups):
        wanted = [bases[group] + j for j in range(each - KMAX)]
        if group % CHIPS > 0:
            wanted += [bases[group - 1] + each - KMAX + k for k in range(KMAX)]
        hit = jnp.zeros((1, LANES), f32)
        for index in wanted:
            hit = jnp.where(lane == table[index], 1.0, hit)
        need.append(hit)
        need_ref[group : group + 1, :] = hit
    for part in range(2):
        for chip in range(CHIPS):
            come = (chip - (lane >> 4)) & (CHIPS - 1)
            reach = jnp.zeros((1, LANES), f32)
            for hops in range(1, CHIPS):
                there = need[part * CHIPS + (chip + hops) % CHIPS] > 0
                reach = jnp.where(there & (come + hops < CHIPS), float(hops), reach)
            row = part * CHIPS + chip
            far_ref[row : row + 1, :] = reach

    row = lax.broadcasted_iota(jnp.int32, (groups, LANES), 0)
    entry = lax.broadcasted_iota(jnp.int32, (groups, LANES), 1)
    chip, owner, slot = row & (CHIPS - 1), entry >> 4, entry & (ENTRIES_EACH - 1)
    loc = jnp.where(owner == chip, slot, -1).astype(f32)
    sent = jnp.where(owner == chip, 1.0, 0.0)
    from_behind = owner == ((chip + CHIPS - 1) & (CHIPS - 1))
    halves = [from_behind & (slot < HALF), from_behind & (slot >= HALF)]
    flights = [jnp.where(half, slot + ENTRIES_EACH, -1).astype(f32) for half in halves]
    far, needed = far_ref[...], need_ref[...]
    swept = jnp.zeros((groups, LANES), f32)
    slot_of = jnp.zeros((groups, LANES), f32)
    lists = jnp.full((groups, LANES), -1.0, f32)
    picks = jnp.full((groups, LANES), -1.0, f32)
    one, two = lax.broadcasted_iota(jnp.int32, (LANES, LANES), 0), lax.broadcasted_iota(jnp.int32, (LANES, LANES), 1)
    earlier = jnp.where(one < two, 1.0, 0.0).astype(jnp.bfloat16)
    to, source = lax.broadcasted_iota(jnp.int32, (groups, groups), 0), lax.broadcasted_iota(jnp.int32, (groups, groups), 1)
    behind = jnp.where(to & (CHIPS - 1) == 0, to + CHIPS - 1, to - 1)
    step = jnp.where(source == behind, 1.0, 0.0).astype(jnp.bfloat16)

    def ranked(mask):
        return jnp.dot(mask.astype(jnp.bfloat16), earlier, preferred_element_type=f32)

    def listed(into, taken, rank, number, cap):
        for b in range(cap):
            pick = jnp.max(jnp.where((taken > 0) & (rank == b), loc, -1.0), axis=1, keepdims=True)
            into = jnp.where(entry == number * CAP + b, pick, into)
        return into

    for number in range(SWEEPS):
        loc = jnp.maximum(loc, flights[number])
        if number == ROUNDS:
            loc = jnp.maximum(loc, flights[number + 1])
        ready = jnp.where((needed > 0) & (loc >= 0) & (swept == 0), 1.0, 0.0)
        rank = ranked(ready)
        taken = jnp.where((ready > 0) & (rank < SWEPT[number]), 1.0, 0.0)
        swept = swept + taken
        slot_of = slot_of + taken * (rank + number * CAP)
        picks = listed(picks, taken, rank, number, SWEPT[number])
        if number < ROUNDS:
            ready = jnp.where((far > 0) & (loc >= 0) & (sent == 0), 1.0, 0.0)
            rank = jnp.zeros((groups, LANES), f32)
            above = jnp.zeros((groups, 1), f32)
            for hops in range(CHIPS - 1, 0, -1):
                level = jnp.where(far == hops, ready, 0.0)
                rank = jnp.where(far == hops, ranked(level) + above, rank)
                above = above + jnp.sum(level, axis=1, keepdims=True)
            taken = jnp.where((ready > 0) & (rank < CAP), 1.0, 0.0)
            sent = sent + taken
            lists = listed(lists, taken, rank, number, CAP)
            came = jnp.dot(step, (taken * (rank + 1)).astype(jnp.bfloat16), preferred_element_type=f32)
            flights.append(jnp.where(came > 0, came + float(2 * ENTRIES_EACH + number * CAP - 1), -1.0))
    lists_ref[...] = lists
    picks_ref[...] = picks
    slots_ref[...] = slot_of
    missing = jnp.sum(jnp.where((far > 0) & (sent == 0), 1.0, 0.0)) + jnp.sum(
        jnp.where((needed > 0) & (swept == 0), 1.0, 0.0)
    )
    plan_ref[...] = jnp.zeros(plan_ref.shape, jnp.int32)
    for line, rows in enumerate((lists_ref, picks_ref, slots_ref)):
        plan_ref[line : line + 1, :] = rows[pl.ds(me, 1), :].astype(jnp.int32)
    plan_ref[3:4, :] = jnp.full((1, LANES), missing, f32).astype(jnp.int32)


def make_plan(place, table):
    return pl.pallas_call(
        plan_kernel,
        out_shape=jax.ShapeDtypeStruct((8, LANES), jnp.int32),
        in_specs=[pl.BlockSpec(memory_space=pltpu.SMEM)] * 2,
        out_specs=pl.BlockSpec(memory_space=pltpu.VMEM),
        scratch_shapes=[pltpu.VMEM((2 * CHIPS, LANES), jnp.float32)] * 5,
        name="plan",
    )(place, table)


def pack(plan, number, pool):
    lines, caps = ((0, 1), (CAP, CAP)) if number < ROUNDS else ((1,), SWEPT[-1:])
    starts = [0]
    for array in pool:
        starts.append(starts[-1] + array.shape[0])

    def kernel(plan_ref, *refs):
        sources, outs = refs[: len(pool)], refs[len(pool) :]
        for line, out in zip(lines, outs):
            for b in range(out.shape[0]):
                at = plan_ref[line * LANES + number * CAP + b]
                for source, low, high in zip(sources, starts, starts[1:]):

                    @pl.when((at >= low) & (at < high))
                    def _(source=source, low=low, out=out, b=b, at=at):
                        out[b] = source[at - low]

    in_vmem = pl.BlockSpec(memory_space=pltpu.VMEM)
    return pl.pallas_call(
        kernel,
        out_shape=tuple(jax.ShapeDtypeStruct((cap,) + pool[0].shape[1:], pool[0].dtype) for cap in caps),
        grid_spec=pltpu.PrefetchScalarGridSpec(
            num_scalar_prefetch=1, in_specs=[in_vmem] * len(pool), out_specs=(in_vmem,) * len(lines)
        ),
        compiler_params=pltpu.CompilerParams(vmem_limit_bytes=VMEM_LIMIT),
        cost_estimate=LITTLE,
        name="pack",
    )(plan, *pool)


def previous_rows(nbr_owner, nbr_slot, nbr_count):
    rows = jnp.concatenate([nbr_owner, nbr_slot, nbr_count[:, None]], axis=1)
    rows = jnp.concatenate([shifted(rows[-1:], "seq", 1), rows[:-1]], axis=0)
    return rows[:, :KMAX], rows[:, KMAX : 2 * KMAX], rows[:, 2 * KMAX]


def fetch_by_request(store, owners, slots):
    owners_axis = lax.axis_size("seq")
    stretches = owners.shape[0]
    depth = min(stretches, max(2, 2 * stretches * KMAX // owners_axis) + 1)
    owners, slots = owners.reshape(-1), slots.reshape(-1)
    order = jnp.arange(owners.shape[0], dtype=jnp.int32)
    before = (owners[:, None] == owners[None, :]) & (order[None, :] < order[:, None])
    target = owners * depth + jnp.sum(before.astype(jnp.int32), axis=1)
    hits = target[:, None] == jnp.arange(owners_axis * depth, dtype=jnp.int32)[None, :]
    table = jnp.sum(jnp.where(hits, slots[:, None], 0), axis=0).reshape(owners_axis, depth)
    asked = lax.all_to_all(table, "seq", split_axis=0, concat_axis=0, tiled=True)
    arrived = lax.all_to_all(store[asked], "seq", split_axis=0, concat_axis=0, tiled=True)
    fetched = arrived.reshape(owners_axis * depth, NLEN, store.shape[2])[target]
    return lax.all_gather(fetched, FEATURES, axis=2, tiled=True)


def onward(value):
    size = lax.axis_size("seq")
    return lax.ppermute(value, "seq", [(chip, (chip + 1) % size) for chip in range(size)])


def four_pieces(value):
    across = swapped(value, "mp")
    return [value, swapped(value, "rep"), across, swapped(across, "rep")]


def fetch_all(store, owners, slots):
    seq = lax.axis_index("seq")
    everything = [store]
    for distance in range(1, lax.axis_size("seq")):
        for steps in (distance, -distance):
            everything.append(shifted(store, "seq", steps))
    ahead = owners - seq
    place = jnp.where(ahead == 0, 0, jnp.where(ahead < 0, -2 * ahead - 1, 2 * ahead))
    pool = jnp.concatenate(everything, axis=0)
    return pool[(place * store.shape[0] + slots).reshape(-1)]


def places_of_pieces():
    block = 2 * lax.axis_index("mp") + lax.axis_index("rep")
    return jnp.stack([block ^ i for i in range(4)]).astype(jnp.int32)


def every_group(places, groups):
    return jnp.concatenate([places, jnp.ones((groups,), jnp.int32), jnp.arange(groups, dtype=jnp.int32)])


def exchanged_table(codes):
    own_part = [codes]
    for offset in range(1, CHIPS):
        own_part.append(lax.ppermute(codes, "seq", [(chip, chip ^ offset) for chip in range(CHIPS)]))
    own_part = jnp.stack(own_part)
    return jnp.concatenate([own_part, swapped(own_part, "parts")], axis=0)


def streamed(queries, key_weight, value_weight, enc_gain, store, nbr_owner, nbr_slot, nbr_count):
    stretches = nbr_owner.shape[0]
    total = stretches * KMAX
    seq = lax.axis_index("seq")
    me = lax.axis_index("parts") * CHIPS + seq
    kept = jnp.arange(KMAX, dtype=jnp.int32)[None, :] < nbr_count[:, None]
    codes = jnp.where(kept, nbr_owner * ENTRIES_EACH + nbr_slot, -1).reshape(-1)
    first, second, codes, enc_gain = lax.optimization_barrier((store[:HALF], store[HALF:], codes, enc_gain))
    table = exchanged_table(codes)
    flights = [onward(first), onward(second)]
    gain = jnp.concatenate(four_pieces(enc_gain[None]), axis=1)
    plan = make_plan(me.reshape(1).astype(jnp.int32), table.reshape(-1)).reshape(-1)
    missing = plan[3 * LANES]

    offset = jnp.where(seq > 0, (seq ^ (seq - 1)) & 3, 0)
    behind = table[offset]
    asked = jnp.concatenate([jnp.where(seq > 0, behind[total - KMAX :], -1), codes[: total - KMAX]])
    asked = asked.reshape(stretches, KMAX)
    counts = jnp.sum((asked >= 0).astype(jnp.int32), axis=1)
    first = jnp.maximum(asked[:, 0], 0)
    asked = jnp.stack([first, jnp.where(asked[:, 1] >= 0, asked[:, 1], first)], axis=1).reshape(-1)

    places = places_of_pieces()
    room = sum(SWEPT)
    wanted = plan[LANES : LANES + room].reshape(room // GROUP, GROUP)[:, 0] >= 0
    group = jnp.arange(room // GROUP, dtype=jnp.int32)
    latest = jnp.max(jnp.where((group[None, :] <= group[:, None]) & wanted[None, :], group[None, :], 0), axis=1)
    marks = jnp.concatenate([places, wanted.astype(jnp.int32), latest])
    slots = plan[2 * LANES : 3 * LANES][asked]

    pieces, held = [], ()
    for number in range(SWEEPS):
        *ways, mine = pack(plan, number, [store] + flights[: number + 1 if number < ROUNDS else None])
        flights += [onward(way) for way in ways]
        pieces.append([mine, swapped(mine, "rep"), swapped(mine, "mp")])
        if number > 0:
            pieces[number - 1].append(swapped(pieces[number - 1][2], "rep"))
        if number == SWEEPS - 2:
            ripe, pieces[number - 1][2] = lax.optimization_barrier((pieces[:2], pieces[number - 1][2]))
            held = project(marks, gain, ripe, key_weight, value_weight, GROUP, room)
        if number + 1 < SWEEPS:
            across = [parts[2] for parts in pieces[:number]] if number + 2 < SWEEPS else []
            came = slice(number + 1, number + 2 if number + 2 < SWEEPS else None)
            flights[came], across, pieces[number][1], gain, slots, marks, held = lax.optimization_barrier(
                (flights[came], across, pieces[number][1], gain, slots, marks, held)
            )
            for parts, arrived in zip(pieces, across):
                parts[2] = arrived
    ripe, _ = lax.optimization_barrier((pieces[2:-1], mine))
    held = project(marks, gain, ripe, key_weight, value_weight, GROUP, room, 2 * CAP // GROUP, held)
    late, held = lax.optimization_barrier((pieces[-1], held))
    late = [*late, swapped(late[2], "rep")]
    done = (SWEEPS - 1) * CAP // GROUP
    keys, values = project(marks, gain, [late], key_weight, value_weight, GROUP, room, done, held)

    def whole(state):
        mine = fetch_all(store, asked >> 4, asked & (ENTRIES_EACH - 1))
        marks = every_group(places, room // 4)
        keys, values = project(marks, gain, [four_pieces(mine)], key_weight, value_weight, 4, room)
        return jnp.zeros_like(state[0]), jnp.arange(total, dtype=jnp.int32), keys, values

    state = lax.while_loop(lambda state: state[0] > 0, whole, (missing, slots, keys, values))
    return attend(state[1], counts, queries, *state[2:])


def requested(queries, key_weight, value_weight, enc_gain, store, nbr_owner, nbr_slot, nbr_count):
    gain = lax.all_gather(enc_gain, FEATURES, axis=0, tiled=True)[None]
    owners, slots, counts = previous_rows(nbr_owner, nbr_slot, nbr_count)
    total = owners.size
    pieces = [fetch_by_request(store, owners, slots)]
    marks = every_group(jnp.zeros((1,), jnp.int32), total // 4)
    keys, values = project(marks, gain, [pieces], key_weight, value_weight, 4, total)
    return attend(jnp.arange(total, dtype=jnp.int32), counts, queries, keys, values)


def solution(mesh):
    in_specs = (
        P(SEQ_SPEC, FEATURES),
        P(None, FEATURES),
        P(None, FEATURES),
        P(FEATURES),
        P(SEQ_SPEC, None, FEATURES),
        P(SEQ_SPEC, None),
        P(SEQ_SPEC, None),
        P(SEQ_SPEC),
    )
    out_specs = P(SEQ_SPEC, FEATURES)
    shape = dict(mesh.shape)
    small = shape == {"parts": 2, "seq": CHIPS, "mp": 2, "rep": 2}
    body = streamed if small else requested
    return jax.shard_map(body, mesh=mesh, in_specs=in_specs, out_specs=out_specs, check_vma=False)
```

profile of v0, /device:TPU:0, one launch (start us, length us, event | category | flops | bytes accessed | tf_op | source)
XLA Modules:
  0.0 113.1 jit_solution(9189610385252800749)
XLA Ops:
  2.2 5.1 %collective-permute-start.11 = (s32[24]{0:T(128)S(1)}, s32[24]{0:T(128)S(1)}, u32[]{:S(2)}, u32[]{:S(2)}) collective-permute-start(s32[24]{0:T(128)S(1)} %reshape.130), channel_id=1, source_target_pairs={{0,12},{4,8},{8,4},{12,0},{1,13},{5,9},{9,5},{13,1},{2,14},{6,10},... | collective-permute-start | bytes 296 | tf_op jit(solution)/shard_map/ppermute | solution.py:381
  7.9 1.6 %collective-permute-start.17 = (f32[1,256]{1,0:T(1,128)}, f32[1,256]{1,0:T(1,128)S(1)}, u32[]{:S(2)}, u32[]{:S(2)}) collective-permute-start(f32[1,256]{1,0:T(1,128)} %bitcast.39), channel_id=1, source_target_pairs={{0,2},{2,0},{1,3},{3,1},{4,6},{6,4},{5,7},{7,5},{8,10},{10,8},{9,1... | collective-permute-start | bytes 3080 | tf_op jit(solution)/shard_map/ppermute | solution.py:41
  11.7 1.6 %collective-permute-start.12 = (s32[4,24]{1,0:T(4,128)S(1)}, s32[4,24]{1,0:T(4,128)S(1)}, u32[]{:S(2)}, u32[]{:S(2)}) collective-permute-start(s32[4,24]{1,0:T(4,128)S(1)} %pad_add_fusion.2), channel_id=1, source_target_pairs={{0,16},{16,0},{1,17},{17,1},{2,18},{18,2},{3,19},{19,3},{4,20},{20... | collective-permute-start | bytes 1160 | tf_op jit(solution)/shard_map/ppermute | solution.py:41
  13.9 1.5 %collective-permute-done.12 = s32[4,24]{1,0:T(4,128)S(1)} collective-permute-done((s32[4,24]{1,0:T(4,128)S(1)}, s32[4,24]{1,0:T(4,128)S(1)}, u32[]{:S(2)}, u32[]{:S(2)}) %collective-permute-start.12) | collective-permute-done | bytes 416 | tf_op jit(solution)/shard_map/ppermute | solution.py:41
  16.5 2.5 %plan.1 = s32[8,128]{1,0:T(8,128)} custom-call(s32[1]{0:T(128)} %bitcast.2.place, s32[192]{0:T(256)} %reshape.131.table), custom_call_target="tpu_custom_call" | custom-call | tf_op jit(solution)/shard_map/plan/pallas_call | solution.py:285
  20.9 5.2 %collective-permute-done.13.refs_1_ = bf16[8,128,256]{2,1,0:T(8,128)(2,1)S(1)} collective-permute-done((bf16[8,128,256]{2,1,0:T(8,128)(2,1)S(1)}, bf16[8,128,256]{2,1,0:T(8,128)(2,1)S(1)}, u32[]{:S(2)}, u32[]{:S(2)}) %collective-permute-start.13) | collective-permute-done | bytes 524320 | tf_op jit(solution)/shard_map/ppermute | solution.py:349
  26.8 1.9 %pack.6 = (bf16[4,128,256]{2,1,0:T(8,128)(2,1)S(1)}, bf16[4,128,256]{2,1,0:T(8,128)(2,1)S(1)}) custom-call(s32[1024]{0:T(1024)S(1)} %bitcast.23, bf16[16,128,256]{2,1,0:T(8,128)(2,1)} %refs_0_.11, bf16[8,128,256]{2,1,0:T(8,128)(2,1)S(1)} %collective-permute-done.13.refs_1_), custom_call_target="tpu_custom_call" | custom-call | flops 1 | bytes 1 | tf_op jit(solution)/shard_map/pack/pallas_call | solution.py:313
  32.5 4.8 %collective-permute-done.14.refs_2_ = bf16[8,128,256]{2,1,0:T(8,128)(2,1)S(1)} collective-permute-done((bf16[8,128,256]{2,1,0:T(8,128)(2,1)S(1)}, bf16[8,128,256]{2,1,0:T(8,128)(2,1)S(1)}, u32[]{:S(2)}, u32[]{:S(2)}) %collective-permute-start.14) | collective-permute-done | bytes 524320 | tf_op jit(solution)/shard_map/ppermute | solution.py:349
  38.0 2.0 %pack.7 = (bf16[4,128,256]{2,1,0:T(8,128)(2,1)S(1)}, bf16[4,128,256]{2,1,0:T(8,128)(2,1)S(1)}) custom-call(s32[1024]{0:T(1024)S(1)} %bitcast.24, bf16[16,128,256]{2,1,0:T(8,128)(2,1)} %refs_0_.11, bf16[8,128,256]{2,1,0:T(8,128)(2,1)S(1)} %collective-permute-done.13.refs_1_, bf16[8,128,256]{2,1,0:T(8,128)(2,1)S(1)} %collective-permute-done.14.refs_2_), custom_call_target="tpu_custom_call" | custom-call | flops 1 | bytes 1 | tf_op jit(solution)/shard_map/pack/pallas_call | solution.py:313
  40.3 2.3 %collective-permute-done.19.refs_3_ = bf16[4,128,256]{2,1,0:T(8,128)(2,1)S(1)} collective-permute-done((bf16[4,128,256]{2,1,0:T(8,128)(2,1)S(1)}, bf16[4,128,256]{2,1,0:T(8,128)(2,1)S(1)}, u32[]{:S(2)}, u32[]{:S(2)}) %collective-permute-start.19) | collective-permute-done | bytes 262176 | tf_op jit(solution)/shard_map/ppermute | solution.py:349
  42.6 1.9 %pack.8 = (bf16[4,128,256]{2,1,0:T(8,128)(2,1)S(1)}, bf16[4,128,256]{2,1,0:T(8,128)(2,1)S(1)}) custom-call(s32[1024]{0:T(1024)S(1)} %bitcast.25, bf16[16,128,256]{2,1,0:T(8,128)(2,1)} %refs_0_.11, bf16[8,128,256]{2,1,0:T(8,128)(2,1)S(1)} %collective-permute-done.13.refs_1_, bf16[8,128,256]{2,1,0:T(8,128)(2,1)S(1)} %collective-permute-done.14.refs_2_, ...), custom_call_target="tpu_custom_call" | custom-call | flops 1 | bytes 1 | tf_op jit(solution)/shard_map/pack/pallas_call | solution.py:313
  45.4 5.7 %collective-permute-done.22.refs_4_ = bf16[4,128,256]{2,1,0:T(8,128)(2,1)S(1)} collective-permute-done((bf16[4,128,256]{2,1,0:T(8,128)(2,1)S(1)}, bf16[4,128,256]{2,1,0:T(8,128)(2,1)S(1)}, u32[]{:S(2)}, u32[]{:S(2)}) %collective-permute-start.22) | collective-permute-done | bytes 262176 | tf_op jit(solution)/shard_map/ppermute | solution.py:349
  51.8 2.0 %pack.9 = (bf16[4,128,256]{2,1,0:T(8,128)(2,1)S(1)}, bf16[4,128,256]{2,1,0:T(8,128)(2,1)S(1)}) custom-call(s32[1024]{0:T(1024)S(1)} %bitcast.26, bf16[16,128,256]{2,1,0:T(8,128)(2,1)} %refs_0_.11, bf16[8,128,256]{2,1,0:T(8,128)(2,1)S(1)} %collective-permute-done.13.refs_1_, bf16[8,128,256]{2,1,0:T(8,128)(2,1)S(1)} %collective-permute-done.14.refs_2_, ...), custom_call_target="tpu_custom_call" | custom-call | flops 1 | bytes 1 | tf_op jit(solution)/shard_map/pack/pallas_call | solution.py:313
  54.5 1.7 %collective-permute-done.26.refs_5_ = bf16[4,128,256]{2,1,0:T(8,128)(2,1)S(1)} collective-permute-done((bf16[4,128,256]{2,1,0:T(8,128)(2,1)S(1)}, bf16[4,128,256]{2,1,0:T(8,128)(2,1)S(1)}, u32[]{:S(2)}, u32[]{:S(2)}) %collective-permute-start.26) | collective-permute-done | bytes 262176 | tf_op jit(solution)/shard_map/ppermute | solution.py:349
  56.2 1.8 %collective-permute-start.33 = (bf16[4,128,256]{2,1,0:T(8,128)(2,1)S(1)}, bf16[4,128,256]{2,1,0:T(8,128)(2,1)S(1)}, u32[]{:S(2)}, u32[]{:S(2)}) collective-permute-start(bf16[4,128,256]{2,1,0:T(8,128)(2,1)S(1)} %get-tuple-element.198.refs_4_), channel_id=1, source_target_pairs={{0,2},{2,0},{1,3},{3,1},{4,6},{6,4},{5,7},{7,5},{8,10},{10,8},{9,1... | collective-permute-start | bytes 786440 | tf_op jit(solution)/shard_map/ppermute | solution.py:41
  58.0 1.9 %pack.10 = (bf16[4,128,256]{2,1,0:T(8,128)(2,1)S(1)}, bf16[4,128,256]{2,1,0:T(8,128)(2,1)S(1)}) custom-call(s32[1024]{0:T(1024)S(1)} %bitcast.27, bf16[16,128,256]{2,1,0:T(8,128)(2,1)} %refs_0_.11, bf16[8,128,256]{2,1,0:T(8,128)(2,1)S(1)} %collective-permute-done.13.refs_1_, bf16[8,128,256]{2,1,0:T(8,128)(2,1)S(1)} %collective-permute-done.14.refs_2_, ...), custom_call_target="tpu_custom_call" | custom-call | flops 1 | bytes 1 | tf_op jit(solution)/shard_map/pack/pallas_call | solution.py:313
  60.4 4.3 %collective-permute-done.33.refs_6_ = bf16[4,128,256]{2,1,0:T(8,128)(2,1)S(1)} collective-permute-done((bf16[4,128,256]{2,1,0:T(8,128)(2,1)S(1)}, bf16[4,128,256]{2,1,0:T(8,128)(2,1)S(1)}, u32[]{:S(2)}, u32[]{:S(2)}) %collective-permute-start.33) | collective-permute-done | bytes 262176 | tf_op jit(solution)/shard_map/ppermute | solution.py:41
  64.7 9.7 %project.5 = (bf16[28,128,1024]{2,1,0:T(8,128)(2,1)S(1)}, bf16[28,128,1024]{2,1,0:T(8,128)(2,1)}) custom-call(s32[32]{0:T(128)S(1)} %concatenate.23.marks_ref, f32[1,1024]{1,0:T(1,128)S(1)} %pad_maximum_fusion.gain_ref, bf16[4,128,256]{2,1,0:T(8,128)(2,1)S(1)} %get-tuple-element.174.refs_0_, bf16[4,128,256]{2,1,0:T(8,128)(2,1)S(1)} %collective-permute-done.15.refs_1_, ...), custom_call_target="tpu_custom_call" | custom-call | flops 1 | bytes 1 | tf_op jit(solution)/shard_map/project/pallas_call | solution.py:102
  74.4 1.8 %pack.11.refs_0_ = bf16[8,128,256]{2,1,0:T(8,128)(2,1)S(1)} custom-call(s32[1024]{0:T(1024)S(1)} %bitcast.28, bf16[16,128,256]{2,1,0:T(8,128)(2,1)} %refs_0_.11, bf16[8,128,256]{2,1,0:T(8,128)(2,1)S(1)} %collective-permute-done.13.refs_1_, bf16[8,128,256]{2,1,0:T(8,128)(2,1)S(1)} %collective-permute-done.14.refs_2_, ...), custom_call_target="tpu_custom_call" | custom-call | flops 1 | bytes 1 | tf_op jit(solution)/shard_map/pack/pallas_call | solution.py:313
  76.2 2.5 %collective-permute-start.35 = (bf16[8,128,256]{2,1,0:T(8,128)(2,1)S(1)}, bf16[8,128,256]{2,1,0:T(8,128)(2,1)S(1)}, u32[]{:S(2)}, u32[]{:S(2)}) collective-permute-start(bf16[8,128,256]{2,1,0:T(8,128)(2,1)S(1)} %pack.11.refs_0_), channel_id=1, source_target_pairs={{0,2},{2,0},{1,3},{3,1},{4,6},{6,4},{5,7},{7,5},{8,10},{10,8},{9,1... | collective-permute-start | bytes 1572872 | tf_op jit(solution)/shard_map/ppermute | solution.py:41
  81.8 11.4 %project.6 = (bf16[28,128,1024]{2,1,0:T(8,128)(2,1)S(1)}, bf16[28,128,1024]{2,1,0:T(8,128)(2,1)}) custom-call(s32[32]{0:T(128)S(1)} %concatenate.23.marks_ref, f32[1,1024]{1,0:T(1,128)S(1)} %pad_maximum_fusion.gain_ref, bf16[4,128,256]{2,1,0:T(8,128)(2,1)S(1)} %get-tuple-element.194.refs_0_, ...), custom_call_target="tpu_custom_call", output_to_operand_aliasing={{0}: (16, {}), {1}: (17, {})} | custom-call | flops 1 | bytes 1 | tf_op jit(solution)/shard_map/project/pallas_call | solution.py:102
  93.2 2.9 %copy-done.4 = bf16[28,128,1024]{2,1,0:T(8,128)(2,1)} copy-done((bf16[28,128,1024]{2,1,0:T(8,128)(2,1)}, bf16[28,128,1024]{2,1,0:T(8,128)(2,1)S(1)}, u32[]{:S(2)}) %copy-start.4) | copy-done | bytes 7340056
  98.0 3.8 %project.7 = (bf16[28,128,1024]{2,1,0:T(8,128)(2,1)}, bf16[28,128,1024]{2,1,0:T(8,128)(2,1)}) custom-call(s32[32]{0:T(128)S(1)} %concatenate.23.marks_ref, f32[1,1024]{1,0:T(1,128)S(1)} %pad_maximum_fusion.gain_ref, bf16[8,128,256]{2,1,0:T(8,128)(2,1)S(1)} %pack.11.refs_0_, ...), custom_call_target="tpu_custom_call", output_to_operand_aliasing={{0}: (8, {}), {1}: (9, {})} | custom-call | flops 1 | bytes 1 | tf_op jit(solution)/shard_map/project/pallas_call | solution.py:102
  102.6 10.4 %attend.1 = bf16[768,1024]{1,0:T(8,128)(2,1)} custom-call(s32[24]{0:T(128)} %get-tuple-element.217.slots, s32[12]{0:T(128)} %convert_reduce_fusion.counts, bf16[768,1024]{1,0:T(8,128)(2,1)} %query_ref.1, bf16[28,128,1024]{2,1,0:T(8,128)(2,1)} %get-tuple-element.218.refs_0_.refs_1_.refs_2_.refs_3_.refs_4_.refs_5_, ...), custom_call_target="tpu_custom_call" | custom-call | flops 1 | bytes 1 | tf_op jit(solution)/shard_map/attend/pallas_call | solution.py:178
  (90 shorter events, 22.5 us)
Async XLA Ops:
  2.2 7.4 %collective-permute-start.11 = (s32[24]{0:T(128)S(1)}, s32[24]{0:T(128)S(1)}, u32[]{:S(2)}, u32[]{:S(2)}) collective-permute-start(s32[24]{0:T(128)S(1)} %reshape.130), channel_id=1, source_target_pairs={{0,12},{4,8},{8,4},{12,0},{1,13},{5,9},{9,5},{13,1},{2,14},{6,10},... | collective-permute-start | bytes 296 | tf_op jit(solution)/shard_map/ppermute | solution.py:381
  7.3 4.4 %collective-permute-start.10 = (s32[24]{0:T(128)S(1)}, s32[24]{0:T(128)S(1)}, u32[]{:S(2)}, u32[]{:S(2)}) collective-permute-start(s32[24]{0:T(128)S(1)} %reshape.130), channel_id=1, source_target_pairs={{0,8},{4,12},{8,0},{12,4},{1,9},{5,13},{9,1},{13,5},{2,10},{6,14},... | collective-permute-start | bytes 296 | tf_op jit(solution)/shard_map/ppermute | solution.py:381
  7.3 4.4 %collective-permute-start.9 = (s32[24]{0:T(128)S(1)}, s32[24]{0:T(128)S(1)}, u32[]{:S(2)}, u32[]{:S(2)}) collective-permute-start(s32[24]{0:T(128)S(1)} %reshape.130), channel_id=1, source_target_pairs={{0,4},{4,0},{8,12},{12,8},{1,5},{5,1},{9,13},{13,9},{2,6},{6,2},{1... | collective-permute-start | bytes 296 | tf_op jit(solution)/shard_map/ppermute | solution.py:381
  7.9 21.0 %collective-permute-start.17 = (f32[1,256]{1,0:T(1,128)}, f32[1,256]{1,0:T(1,128)S(1)}, u32[]{:S(2)}, u32[]{:S(2)}) collective-permute-start(f32[1,256]{1,0:T(1,128)} %bitcast.39), channel_id=1, source_target_pairs={{0,2},{2,0},{1,3},{3,1},{4,6},{6,4},{5,7},{7,5},{8,10},{10,8},{9,1... | collective-permute-start | bytes 3080 | tf_op jit(solution)/shard_map/ppermute | solution.py:41
  9.6 21.3 %collective-permute-start.16 = (f32[1,256]{1,0:T(1,128)}, f32[1,256]{1,0:T(1,128)S(1)}, u32[]{:S(2)}, u32[]{:S(2)}) collective-permute-start(f32[1,256]{1,0:T(1,128)} %bitcast.40), channel_id=1, source_target_pairs={{0,1},{1,0},{2,3},{3,2},{4,5},{5,4},{6,7},{7,6},{8,9},{9,8},{10,11... | collective-permute-start | bytes 3080 | tf_op jit(solution)/shard_map/ppermute | solution.py:41
  9.6 16.5 %collective-permute-start.13 = (bf16[8,128,256]{2,1,0:T(8,128)(2,1)S(1)}, bf16[8,128,256]{2,1,0:T(8,128)(2,1)S(1)}, u32[]{:S(2)}, u32[]{:S(2)}) collective-permute-start(bf16[8,128,256]{2,1,0:T(8,128)(2,1)S(1)} %get-tuple-element.138), channel_id=1, source_target_pairs={{0,4},{4,8},{8,12},{12,0},{1,5},{5,9},{9,13},{13,1},{2,6},{6,10},{... | collective-permute-start | bytes 1572872 | tf_op jit(solution)/shard_map/ppermute | solution.py:349
  13.3 24.0 %collective-permute-start.14 = (bf16[8,128,256]{2,1,0:T(8,128)(2,1)S(1)}, bf16[8,128,256]{2,1,0:T(8,128)(2,1)S(1)}, u32[]{:S(2)}, u32[]{:S(2)}) collective-permute-start(bf16[8,128,256]{2,1,0:T(8,128)(2,1)S(1)} %get-tuple-element.139), channel_id=1, source_target_pairs={{0,4},{4,8},{8,12},{12,0},{1,5},{5,9},{9,13},{13,1},{2,6},{6,10},{... | collective-permute-start | bytes 1572872 | tf_op jit(solution)/shard_map/ppermute | solution.py:349
  28.7 8.6 %collective-permute-start.15 = (bf16[4,128,256]{2,1,0:T(8,128)(2,1)S(1)}, bf16[4,128,256]{2,1,0:T(8,128)(2,1)S(1)}, u32[]{:S(2)}, u32[]{:S(2)}) collective-permute-start(bf16[4,128,256]{2,1,0:T(8,128)(2,1)S(1)} %get-tuple-element.174.refs_0_), channel_id=1, source_target_pairs={{0,1},{1,0},{2,3},{3,2},{4,5},{5,4},{6,7},{7,6},{8,9},{9,8},{10,11... | collective-permute-start | bytes 786440 | tf_op jit(solution)/shard_map/ppermute | solution.py:41
  31.5 11.1 %collective-permute-start.20 = (bf16[4,128,256]{2,1,0:T(8,128)(2,1)S(1)}, bf16[4,128,256]{2,1,0:T(8,128)(2,1)S(1)}, u32[]{:S(2)}, u32[]{:S(2)}) collective-permute-start(bf16[4,128,256]{2,1,0:T(8,128)(2,1)S(1)} %get-tuple-element.174.refs_0_), channel_id=1, source_target_pairs={{0,2},{2,0},{1,3},{3,1},{4,6},{6,4},{5,7},{7,5},{8,10},{10,8},{9,1... | collective-permute-start | bytes 786440 | tf_op jit(solution)/shard_map/ppermute | solution.py:41
  32.5 10.1 %collective-permute-start.19 = (bf16[4,128,256]{2,1,0:T(8,128)(2,1)S(1)}, bf16[4,128,256]{2,1,0:T(8,128)(2,1)S(1)}, u32[]{:S(2)}, u32[]{:S(2)}) collective-permute-start(bf16[4,128,256]{2,1,0:T(8,128)(2,1)S(1)} %get-tuple-element.143), channel_id=1, source_target_pairs={{0,4},{4,8},{8,12},{12,0},{1,5},{5,9},{9,13},{13,1},{2,6},{6,10},{... | collective-permute-start | bytes 786440 | tf_op jit(solution)/shard_map/ppermute | solution.py:349
  40.0 11.1 %collective-permute-start.23 = (bf16[4,128,256]{2,1,0:T(8,128)(2,1)S(1)}, bf16[4,128,256]{2,1,0:T(8,128)(2,1)S(1)}, u32[]{:S(2)}, u32[]{:S(2)}) collective-permute-start(bf16[4,128,256]{2,1,0:T(8,128)(2,1)S(1)} %get-tuple-element.178.refs_4_), channel_id=1, source_target_pairs={{0,2},{2,0},{1,3},{3,1},{4,6},{6,4},{5,7},{7,5},{8,10},{10,8},{9,1... | collective-permute-start | bytes 786440 | tf_op jit(solution)/shard_map/ppermute | solution.py:41
  40.3 10.8 %collective-permute-start.22 = (bf16[4,128,256]{2,1,0:T(8,128)(2,1)S(1)}, bf16[4,128,256]{2,1,0:T(8,128)(2,1)S(1)}, u32[]{:S(2)}, u32[]{:S(2)}) collective-permute-start(bf16[4,128,256]{2,1,0:T(8,128)(2,1)S(1)} %get-tuple-element.149), channel_id=1, source_target_pairs={{0,4},{4,8},{8,12},{12,0},{1,5},{5,9},{9,13},{13,1},{2,6},{6,10},{... | collective-permute-start | bytes 786440 | tf_op jit(solution)/shard_map/ppermute | solution.py:349
  44.5 6.6 %collective-permute-start.24 = (bf16[4,128,256]{2,1,0:T(8,128)(2,1)S(1)}, bf16[4,128,256]{2,1,0:T(8,128)(2,1)S(1)}, u32[]{:S(2)}, u32[]{:S(2)}) collective-permute-start(bf16[4,128,256]{2,1,0:T(8,128)(2,1)S(1)} %get-tuple-element.194.refs_0_), channel_id=1, source_target_pairs={{0,1},{1,0},{2,3},{3,2},{4,5},{5,4},{6,7},{7,6},{8,9},{9,8},{10,11... | collective-permute-start | bytes 786440 | tf_op jit(solution)/shard_map/ppermute | solution.py:41
  44.6 13.3 %collective-permute-start.27 = (bf16[4,128,256]{2,1,0:T(8,128)(2,1)S(1)}, bf16[4,128,256]{2,1,0:T(8,128)(2,1)S(1)}, u32[]{:S(2)}, u32[]{:S(2)}) collective-permute-start(bf16[4,128,256]{2,1,0:T(8,128)(2,1)S(1)} %get-tuple-element.194.refs_0_), channel_id=1, source_target_pairs={{0,2},{2,0},{1,3},{3,1},{4,6},{6,4},{5,7},{7,5},{8,10},{10,8},{9,1... | collective-permute-start | bytes 786440 | tf_op jit(solution)/shard_map/ppermute | solution.py:41
  45.4 10.8 %collective-permute-start.26 = (bf16[4,128,256]{2,1,0:T(8,128)(2,1)S(1)}, bf16[4,128,256]{2,1,0:T(8,128)(2,1)S(1)}, u32[]{:S(2)}, u32[]{:S(2)}) collective-permute-start(bf16[4,128,256]{2,1,0:T(8,128)(2,1)S(1)} %get-tuple-element.157), channel_id=1, source_target_pairs={{0,4},{4,8},{8,12},{12,0},{1,5},{5,9},{9,13},{13,1},{2,6},{6,10},{... | collective-permute-start | bytes 786440 | tf_op jit(solution)/shard_map/ppermute | solution.py:349
  53.9 6.0 %collective-permute-start.31 = (bf16[4,128,256]{2,1,0:T(8,128)(2,1)S(1)}, bf16[4,128,256]{2,1,0:T(8,128)(2,1)S(1)}, u32[]{:S(2)}, u32[]{:S(2)}) collective-permute-start(bf16[4,128,256]{2,1,0:T(8,128)(2,1)S(1)} %collective-permute-done.20.refs_2_), channel_id=1, source_target_pairs={{0,1},{1,0},{2,3},{3,2},{4,5},{5,4},{6,7},{7,6},{8,9},{9,8},{10,11... | collective-permute-start | bytes 786440 | tf_op jit(solution)/shard_map/ppermute | solution.py:41
  54.4 5.6 %collective-permute-start.32 = (bf16[4,128,256]{2,1,0:T(8,128)(2,1)S(1)}, bf16[4,128,256]{2,1,0:T(8,128)(2,1)S(1)}, u32[]{:S(2)}, u32[]{:S(2)}) collective-permute-start(bf16[4,128,256]{2,1,0:T(8,128)(2,1)S(1)} %collective-permute-done.23.refs_6_), channel_id=1, source_target_pairs={{0,1},{1,0},{2,3},{3,2},{4,5},{5,4},{6,7},{7,6},{8,9},{9,8},{10,11... | collective-permute-start | bytes 786440 | tf_op jit(solution)/shard_map/ppermute | solution.py:41
  56.2 8.5 %collective-permute-start.33 = (bf16[4,128,256]{2,1,0:T(8,128)(2,1)S(1)}, bf16[4,128,256]{2,1,0:T(8,128)(2,1)S(1)}, u32[]{:S(2)}, u32[]{:S(2)}) collective-permute-start(bf16[4,128,256]{2,1,0:T(8,128)(2,1)S(1)} %get-tuple-element.198.refs_4_), channel_id=1, source_target_pairs={{0,2},{2,0},{1,3},{3,1},{4,6},{6,4},{5,7},{7,5},{8,10},{10,8},{9,1... | collective-permute-start | bytes 786440 | tf_op jit(solution)/shard_map/ppermute | solution.py:41
  57.9 16.5 %collective-permute-start.25 = (bf16[4,128,256]{2,1,0:T(8,128)(2,1)S(1)}, bf16[4,128,256]{2,1,0:T(8,128)(2,1)S(1)}, u32[]{:S(2)}, u32[]{:S(2)}) collective-permute-start(bf16[4,128,256]{2,1,0:T(8,128)(2,1)S(1)} %get-tuple-element.156), channel_id=1, source_target_pairs={{0,4},{4,8},{8,12},{12,0},{1,5},{5,9},{9,13},{13,1},{2,6},{6,10},{... | collective-permute-start | bytes 786440 | tf_op jit(solution)/shard_map/ppermute | solution.py:349
  59.9 14.5 %collective-permute-start.29 = (bf16[4,128,256]{2,1,0:T(8,128)(2,1)S(1)}, bf16[4,128,256]{2,1,0:T(8,128)(2,1)S(1)}, u32[]{:S(2)}, u32[]{:S(2)}) collective-permute-start(bf16[4,128,256]{2,1,0:T(8,128)(2,1)S(1)} %get-tuple-element.165), channel_id=1, source_target_pairs={{0,4},{4,8},{8,12},{12,0},{1,5},{5,9},{9,13},{13,1},{2,6},{6,10},{... | collective-permute-start | bytes 786440 | tf_op jit(solution)/shard_map/ppermute | solution.py:349
  59.9 14.5 %collective-permute-start.30 = (bf16[4,128,256]{2,1,0:T(8,128)(2,1)S(1)}, bf16[4,128,256]{2,1,0:T(8,128)(2,1)S(1)}, u32[]{:S(2)}, u32[]{:S(2)}) collective-permute-start(bf16[4,128,256]{2,1,0:T(8,128)(2,1)S(1)} %get-tuple-element.202.refs_8_), channel_id=1, source_target_pairs={{0,1},{1,0},{2,3},{3,2},{4,5},{5,4},{6,7},{7,6},{8,9},{9,8},{10,11... | collective-permute-start | bytes 786440 | tf_op jit(solution)/shard_map/ppermute | solution.py:41
  60.0 19.2 %collective-permute-start.38 = (bf16[4,128,256]{2,1,0:T(8,128)(2,1)S(1)}, bf16[4,128,256]{2,1,0:T(8,128)(2,1)S(1)}, u32[]{:S(2)}, u32[]{:S(2)}) collective-permute-start(bf16[4,128,256]{2,1,0:T(8,128)(2,1)S(1)} %get-tuple-element.202.refs_8_), channel_id=1, source_target_pairs={{0,2},{2,0},{1,3},{3,1},{4,6},{6,4},{5,7},{7,5},{8,10},{10,8},{9,1... | collective-permute-start | bytes 786440 | tf_op jit(solution)/shard_map/ppermute | solution.py:41
  76.2 16.9 %collective-permute-start.35 = (bf16[8,128,256]{2,1,0:T(8,128)(2,1)S(1)}, bf16[8,128,256]{2,1,0:T(8,128)(2,1)S(1)}, u32[]{:S(2)}, u32[]{:S(2)}) collective-permute-start(bf16[8,128,256]{2,1,0:T(8,128)(2,1)S(1)} %pack.11.refs_0_), channel_id=1, source_target_pairs={{0,2},{2,0},{1,3},{3,1},{4,6},{6,4},{5,7},{7,5},{8,10},{10,8},{9,1... | collective-permute-start | bytes 1572872 | tf_op jit(solution)/shard_map/ppermute | solution.py:41
  78.7 14.5 %collective-permute-start.34 = (bf16[8,128,256]{2,1,0:T(8,128)(2,1)S(1)}, bf16[8,128,256]{2,1,0:T(8,128)(2,1)S(1)}, u32[]{:S(2)}, u32[]{:S(2)}) collective-permute-start(bf16[8,128,256]{2,1,0:T(8,128)(2,1)S(1)} %pack.11.refs_0_), channel_id=1, source_target_pairs={{0,1},{1,0},{2,3},{3,2},{4,5},{5,4},{6,7},{7,6},{8,9},{9,8},{10,11... | collective-permute-start | bytes 1572872 | tf_op jit(solution)/shard_map/ppermute | solution.py:41
  (13 other events, 65.0 us)
where the time goes:
time: 113 us
  Pallas kernels  49.4 us (44%)
  waiting for transfers between devices  28.9 us (26%)
  starting transfers between devices  20.1 us (18%)
  local copies, waits for them, and re-layouts  10.8 us (10%)
  other arithmetic  2.68 us (2%)
    pallas_call x3, Pallas kernels, project(): pl.pallas_call(kernel, out_shape=(out, out), grid_spec=pltpu.PrefetchScal...  24.9 us
    ppermute x7, waiting for transfers between devices, onward(): lax.ppermute(value, 'seq', [(chip, (chip + 1) % size) for chip in range(s...  19.7 us
    ppermute x22, starting transfers between devices, swapped(): return lax.ppermute(value, axis, [(0, 1), (1, 0)])  12.5 us
    pallas_call x6, Pallas kernels, pack(): pl.pallas_call(kernel, out_shape=tuple((jax.ShapeDtypeStruct((cap,) + poo...  11.6 us
    pallas_call x1, Pallas kernels, attend(): pl.pallas_call(attend_kernel, out_shape=jax.ShapeDtypeStruct(queries.shap...  10.4 us
    ppermute x22, waiting for transfers between devices, swapped(): return lax.ppermute(value, axis, [(0, 1), (1, 0)])  8.34 us
    ppermute x3, starting transfers between devices, exchanged_table(): lax.ppermute(codes, 'seq', [(chip, chip ^ offset) for chip in range(CHIPS)])  5.76 us
    unnamed x10, local copies, waits for them, and re-layouts  4.93 us
  transfers between devices with their start and end apart: 32, of which 12 were waited for; matrix products, arithmetic and copies ran while one was open for 6% of the time, Pallas kernels for 31%

commit v1 on v0

--- a/solution.py
+++ b/solution.py
@@ -16,7 +16,7 @@
 
 SEQ_SPEC = ("parts", "seq")
 FEATURES = ("mp", "rep")
-VMEM_LIMIT = 28 * 1024 * 1024
+MIB = 1024 * 1024
 
 CHIPS = 4
 ENTRIES_EACH = 16
@@ -114,7 +114,7 @@
             + [pltpu.SemaphoreType.DMA((2 * pieces,))],
         ),
         input_output_aliases={len(operands) - len(held) + i: i for i in range(len(held))},
-        compiler_params=pltpu.CompilerParams(vmem_limit_bytes=47 * 1024 * 1024),
+        compiler_params=pltpu.CompilerParams(vmem_limit_bytes=20 * MIB),
         cost_estimate=LITTLE,
         name="project",
     )(*operands)
@@ -184,7 +184,7 @@
             in_specs=[query_spec] + entries * 2,
             out_specs=query_spec,
         ),
-        compiler_params=pltpu.CompilerParams(vmem_limit_bytes=60 * 1024 * 1024),
+        compiler_params=pltpu.CompilerParams(vmem_limit_bytes=60 * MIB),
         cost_estimate=LITTLE,
         name="attend",
     )(slots, counts, queries, *[keys] * len(entries), *[values] * len(entries))
@@ -316,7 +316,7 @@
         grid_spec=pltpu.PrefetchScalarGridSpec(
             num_scalar_prefetch=1, in_specs=[in_vmem] * len(pool), out_specs=(in_vmem,) * len(lines)
         ),
-        compiler_params=pltpu.CompilerParams(vmem_limit_bytes=VMEM_LIMIT),
+        compiler_params=pltpu.CompilerParams(vmem_limit_bytes=12 * MIB),
         cost_estimate=LITTLE,
         name="pack",
     )(plan, *pool)

time: 113 us -> 112 us (level)
  Pallas kernels: 49.4 us -> 45.9 us
  waiting for transfers between devices: 28.9 us -> 30.6 us
  local copies, waits for them, and re-layouts: 10.8 us -> 12.3 us
    pallas_call x3, Pallas kernels: 24.9 us -> 21.4 us  [project(): pl.pallas_call(kernel, out_shape=(out, out), grid_spec=pltpu.PrefetchScal...]
    unnamed x10 -> x14, local copies, waits for them, and re-layouts: 4.93 us -> 6.55 us
    ppermute x7, waiting for transfers between devices: 19.7 us -> 21.1 us  [onward(): lax.ppermute(value, 'seq', [(chip, (chip + 1) % size) for chip in range(s...]
  transfers between devices with their start and end apart: 32 -> 32, of which waited for: 12 -> 13; matrix products, arithmetic and copies ran while one was open for 6% -> 6% of each run, Pallas kernels for 31% -> 26%
where the time goes in v1:
time: 112 us
  Pallas kernels  45.9 us (41%)
  waiting for transfers between devices  30.6 us (27%)
  starting transfers between devices  19.5 us (17%)
  local copies, waits for them, and re-layouts  12.3 us (11%)
  other arithmetic  2.63 us (2%)
    pallas_call x3, Pallas kernels, project(): pl.pallas_call(kernel, out_shape=(out, out), grid_spec=pltpu.PrefetchScal...  21.4 us
    ppermute x7, waiting for transfers between devices, onward(): lax.ppermute(value, 'seq', [(chip, (chip + 1) % size) for chip in range(s...  21.1 us
    pallas_call x6, Pallas kernels, pack(): pl.pallas_call(kernel, out_shape=tuple((jax.ShapeDtypeStruct((cap,) + poo...  12.1 us
    ppermute x22, starting transfers between devices, swapped(): return lax.ppermute(value, axis, [(0, 1), (1, 0)])  11.9 us
    pallas_call x1, Pallas kernels, attend(): pl.pallas_call(attend_kernel, out_shape=jax.ShapeDtypeStruct(queries.shap...  9.9 us
    ppermute x22, waiting for transfers between devices, swapped(): return lax.ppermute(value, axis, [(0, 1), (1, 0)])  8.55 us
    unnamed x14, local copies, waits for them, and re-layouts  6.55 us
    ppermute x3, starting transfers between devices, exchanged_table(): lax.ppermute(codes, 'seq', [(chip, chip ^ offset) for chip in range(CHIPS)])  5.76 us
  transfers between devices with their start and end apart: 32, of which 13 were waited for; matrix products, arithmetic and copies ran while one was open for 6% of the time, Pallas kernels for 26%

profile of v1, /device:TPU:0, one launch (start us, length us, event | category | flops | bytes accessed | tf_op | source)
XLA Modules:
  0.0 112.1 jit_solution(7228421601437474228)
XLA Ops:
  2.2 5.1 %collective-permute-start.11 = (s32[24]{0:T(128)S(1)}, s32[24]{0:T(128)S(1)}, u32[]{:S(2)}, u32[]{:S(2)}) collective-permute-start(s32[24]{0:T(128)S(1)} %reshape.130), channel_id=1, source_target_pairs={{0,12},{4,8},{8,4},{12,0},{1,13},{5,9},{9,5},{13,1},{2,14},{6,10},... | collective-permute-start | bytes 296 | tf_op jit(solution)/shard_map/ppermute | solution.py:381
  7.9 1.6 %collective-permute-start.17 = (f32[1,256]{1,0:T(1,128)}, f32[1,256]{1,0:T(1,128)S(1)}, u32[]{:S(2)}, u32[]{:S(2)}) collective-permute-start(f32[1,256]{1,0:T(1,128)} %bitcast.39), channel_id=1, source_target_pairs={{0,2},{2,0},{1,3},{3,1},{4,6},{6,4},{5,7},{7,5},{8,10},{10,8},{9,1... | collective-permute-start | bytes 3080 | tf_op jit(solution)/shard_map/ppermute | solution.py:41
  11.7 1.6 %collective-permute-start.12 = (s32[4,24]{1,0:T(4,128)S(1)}, s32[4,24]{1,0:T(4,128)S(1)}, u32[]{:S(2)}, u32[]{:S(2)}) collective-permute-start(s32[4,24]{1,0:T(4,128)S(1)} %pad_add_fusion.2), channel_id=1, source_target_pairs={{0,16},{16,0},{1,17},{17,1},{2,18},{18,2},{3,19},{19,3},{4,20},{20... | collective-permute-start | bytes 1160 | tf_op jit(solution)/shard_map/ppermute | solution.py:41
  16.5 2.5 %plan.1 = s32[8,128]{1,0:T(8,128)} custom-call(s32[1]{0:T(128)} %bitcast.2.place, s32[192]{0:T(256)} %reshape.131.table), custom_call_target="tpu_custom_call" | custom-call | tf_op jit(solution)/shard_map/plan/pallas_call | solution.py:285
  20.8 5.3 %collective-permute-done.13.refs_1_ = bf16[8,128,256]{2,1,0:T(8,128)(2,1)S(1)} collective-permute-done((bf16[8,128,256]{2,1,0:T(8,128)(2,1)S(1)}, bf16[8,128,256]{2,1,0:T(8,128)(2,1)S(1)}, u32[]{:S(2)}, u32[]{:S(2)}) %collective-permute-start.13) | collective-permute-done | bytes 524320 | tf_op jit(solution)/shard_map/ppermute | solution.py:349
  26.8 1.9 %pack.6 = (bf16[4,128,256]{2,1,0:T(8,128)(2,1)S(1)}, bf16[4,128,256]{2,1,0:T(8,128)(2,1)S(1)}) custom-call(s32[1024]{0:T(1024)S(1)} %bitcast.23, bf16[16,128,256]{2,1,0:T(8,128)(2,1)} %refs_0_.11, bf16[8,128,256]{2,1,0:T(8,128)(2,1)S(1)} %collective-permute-done.13.refs_1_), custom_call_target="tpu_custom_call" | custom-call | flops 1 | bytes 1 | tf_op jit(solution)/shard_map/pack/pallas_call | solution.py:313
  32.5 4.8 %collective-permute-done.14.refs_2_ = bf16[8,128,256]{2,1,0:T(8,128)(2,1)S(1)} collective-permute-done((bf16[8,128,256]{2,1,0:T(8,128)(2,1)S(1)}, bf16[8,128,256]{2,1,0:T(8,128)(2,1)S(1)}, u32[]{:S(2)}, u32[]{:S(2)}) %collective-permute-start.14) | collective-permute-done | bytes 524320 | tf_op jit(solution)/shard_map/ppermute | solution.py:349
  38.0 2.3 %pack.7 = (bf16[4,128,256]{2,1,0:T(8,128)(2,1)S(1)}, bf16[4,128,256]{2,1,0:T(8,128)(2,1)S(1)}) custom-call(s32[1024]{0:T(1024)S(1)} %bitcast.24, bf16[16,128,256]{2,1,0:T(8,128)(2,1)} %refs_0_.11, bf16[8,128,256]{2,1,0:T(8,128)(2,1)S(1)} %collective-permute-done.13.refs_1_, bf16[8,128,256]{2,1,0:T(8,128)(2,1)S(1)} %collective-permute-done.14.refs_2_), custom_call_target="tpu_custom_call" | custom-call | flops 1 | bytes 1 | tf_op jit(solution)/shard_map/pack/pallas_call | solution.py:313
  40.6 2.0 %collective-permute-done.19.refs_3_ = bf16[4,128,256]{2,1,0:T(8,128)(2,1)S(1)} collective-permute-done((bf16[4,128,256]{2,1,0:T(8,128)(2,1)S(1)}, bf16[4,128,256]{2,1,0:T(8,128)(2,1)S(1)}, u32[]{:S(2)}, u32[]{:S(2)}) %collective-permute-start.19) | collective-permute-done | bytes 262176 | tf_op jit(solution)/shard_map/ppermute | solution.py:349
  42.6 2.0 %pack.8 = (bf16[4,128,256]{2,1,0:T(8,128)(2,1)S(1)}, bf16[4,128,256]{2,1,0:T(8,128)(2,1)S(1)}) custom-call(s32[1024]{0:T(1024)S(1)} %bitcast.25, bf16[16,128,256]{2,1,0:T(8,128)(2,1)} %refs_0_.11, bf16[8,128,256]{2,1,0:T(8,128)(2,1)S(1)} %collective-permute-done.13.refs_1_, bf16[8,128,256]{2,1,0:T(8,128)(2,1)S(1)} %collective-permute-done.14.refs_2_, ...), custom_call_target="tpu_custom_call" | custom-call | flops 1 | bytes 1 | tf_op jit(solution)/shard_map/pack/pallas_call | solution.py:313
  45.5 6.0 %collective-permute-done.22.refs_4_ = bf16[4,128,256]{2,1,0:T(8,128)(2,1)S(1)} collective-permute-done((bf16[4,128,256]{2,1,0:T(8,128)(2,1)S(1)}, bf16[4,128,256]{2,1,0:T(8,128)(2,1)S(1)}, u32[]{:S(2)}, u32[]{:S(2)}) %collective-permute-start.22) | collective-permute-done | bytes 262176 | tf_op jit(solution)/shard_map/ppermute | solution.py:349
  51.6 1.9 %pack.9 = (bf16[4,128,256]{2,1,0:T(8,128)(2,1)S(1)}, bf16[4,128,256]{2,1,0:T(8,128)(2,1)S(1)}) custom-call(s32[1024]{0:T(1024)S(1)} %bitcast.26, bf16[16,128,256]{2,1,0:T(8,128)(2,1)} %refs_0_.11, bf16[8,128,256]{2,1,0:T(8,128)(2,1)S(1)} %collective-permute-done.13.refs_1_, bf16[8,128,256]{2,1,0:T(8,128)(2,1)S(1)} %collective-permute-done.14.refs_2_, ...), custom_call_target="tpu_custom_call" | custom-call | flops 1 | bytes 1 | tf_op jit(solution)/shard_map/pack/pallas_call | solution.py:313
  54.2 2.3 %collective-permute-done.26.refs_5_ = bf16[4,128,256]{2,1,0:T(8,128)(2,1)S(1)} collective-permute-done((bf16[4,128,256]{2,1,0:T(8,128)(2,1)S(1)}, bf16[4,128,256]{2,1,0:T(8,128)(2,1)S(1)}, u32[]{:S(2)}, u32[]{:S(2)}) %collective-permute-start.26) | collective-permute-done | bytes 262176 | tf_op jit(solution)/shard_map/ppermute | solution.py:349
  56.5 1.8 %collective-permute-start.33 = (bf16[4,128,256]{2,1,0:T(8,128)(2,1)S(1)}, bf16[4,128,256]{2,1,0:T(8,128)(2,1)S(1)}, u32[]{:S(2)}, u32[]{:S(2)}) collective-permute-start(bf16[4,128,256]{2,1,0:T(8,128)(2,1)S(1)} %get-tuple-element.198.refs_4_), channel_id=1, source_target_pairs={{0,2},{2,0},{1,3},{3,1},{4,6},{6,4},{5,7},{7,5},{8,10},{10,8},{9,1... | collective-permute-start | bytes 786440 | tf_op jit(solution)/shard_map/ppermute | solution.py:41
  58.2 1.8 %pack.10 = (bf16[4,128,256]{2,1,0:T(8,128)(2,1)S(1)}, bf16[4,128,256]{2,1,0:T(8,128)(2,1)S(1)}) custom-call(s32[1024]{0:T(1024)S(1)} %bitcast.27, bf16[16,128,256]{2,1,0:T(8,128)(2,1)} %refs_0_.11, bf16[8,128,256]{2,1,0:T(8,128)(2,1)S(1)} %collective-permute-done.13.refs_1_, bf16[8,128,256]{2,1,0:T(8,128)(2,1)S(1)} %collective-permute-done.14.refs_2_, ...), custom_call_target="tpu_custom_call" | custom-call | flops 1 | bytes 1 | tf_op jit(solution)/shard_map/pack/pallas_call | solution.py:313
  60.5 4.5 %collective-permute-done.33.refs_6_ = bf16[4,128,256]{2,1,0:T(8,128)(2,1)S(1)} collective-permute-done((bf16[4,128,256]{2,1,0:T(8,128)(2,1)S(1)}, bf16[4,128,256]{2,1,0:T(8,128)(2,1)S(1)}, u32[]{:S(2)}, u32[]{:S(2)}) %collective-permute-start.33) | collective-permute-done | bytes 262176 | tf_op jit(solution)/shard_map/ppermute | solution.py:41
  65.0 7.2 %project.5 = (bf16[28,128,1024]{2,1,0:T(8,128)(2,1)S(1)}, bf16[28,128,1024]{2,1,0:T(8,128)(2,1)S(1)}) custom-call(s32[32]{0:T(128)S(1)} %concatenate.23.marks_ref, f32[1,1024]{1,0:T(1,128)S(1)} %pad_maximum_fusion.gain_ref, bf16[4,128,256]{2,1,0:T(8,128)(2,1)S(1)} %get-tuple-element.174.refs_0_, bf16[4,128,256]{2,1,0:T(8,128)(2,1)S(1)} %collective-permute-done.15.refs_1_, ...), custom_call_target="tpu_custom_call" | custom-call | flops 1 | bytes 1 | tf_op jit(solution)/shard_map/project/pallas_call | solution.py:102
  72.9 2.1 %pack.11.refs_0_ = bf16[8,128,256]{2,1,0:T(8,128)(2,1)S(1)} custom-call(s32[1024]{0:T(1024)S(1)} %bitcast.28, bf16[16,128,256]{2,1,0:T(8,128)(2,1)} %refs_0_.11, bf16[8,128,256]{2,1,0:T(8,128)(2,1)S(1)} %collective-permute-done.13.refs_1_, bf16[8,128,256]{2,1,0:T(8,128)(2,1)S(1)} %collective-permute-done.14.refs_2_, ...), custom_call_target="tpu_custom_call" | custom-call | flops 1 | bytes 1 | tf_op jit(solution)/shard_map/pack/pallas_call | solution.py:313
  75.1 1.9 %collective-permute-start.35 = (bf16[8,128,256]{2,1,0:T(8,128)(2,1)S(1)}, bf16[8,128,256]{2,1,0:T(8,128)(2,1)S(1)}, u32[]{:S(2)}, u32[]{:S(2)}) collective-permute-start(bf16[8,128,256]{2,1,0:T(8,128)(2,1)S(1)} %pack.11.refs_0_), channel_id=1, source_target_pairs={{0,2},{2,0},{1,3},{3,1},{4,6},{6,4},{5,7},{7,5},{8,10},{10,8},{9,1... | collective-permute-start | bytes 1572872 | tf_op jit(solution)/shard_map/ppermute | solution.py:41
  80.0 7.4 %project.6 = (bf16[28,128,1024]{2,1,0:T(8,128)(2,1)S(1)}, bf16[28,128,1024]{2,1,0:T(8,128)(2,1)S(1)}) custom-call(s32[32]{0:T(128)S(1)} %concatenate.23.marks_ref, f32[1,1024]{1,0:T(1,128)S(1)} %pad_maximum_fusion.gain_ref, bf16[4,128,256]{2,1,0:T(8,128)(2,1)S(1)} %get-tuple-element.194.refs_0_, ...), custom_call_target="tpu_custom_call", output_to_operand_aliasing={{0}: (16, {}), {1}: (17, {})} | custom-call | flops 1 | bytes 1 | tf_op jit(solution)/shard_map/project/pallas_call | solution.py:102
  87.4 2.9 %copy-done.3 = bf16[28,128,1024]{2,1,0:T(8,128)(2,1)} copy-done((bf16[28,128,1024]{2,1,0:T(8,128)(2,1)}, bf16[28,128,1024]{2,1,0:T(8,128)(2,1)S(1)}, u32[]{:S(2)}) %copy-start.3) | copy-done | bytes 7340056
  90.3 2.3 %copy-done.4 = bf16[28,128,1024]{2,1,0:T(8,128)(2,1)} copy-done((bf16[28,128,1024]{2,1,0:T(8,128)(2,1)}, bf16[28,128,1024]{2,1,0:T(8,128)(2,1)S(1)}, u32[]{:S(2)}) %copy-start.4) | copy-done | bytes 7340056
  94.5 6.8 %project.7 = (bf16[28,128,1024]{2,1,0:T(8,128)(2,1)}, bf16[28,128,1024]{2,1,0:T(8,128)(2,1)}) custom-call(s32[32]{0:T(128)S(1)} %concatenate.23.marks_ref, f32[1,1024]{1,0:T(1,128)S(1)} %pad_maximum_fusion.gain_ref, bf16[8,128,256]{2,1,0:T(8,128)(2,1)S(1)} %pack.11.refs_0_, ...), custom_call_target="tpu_custom_call", output_to_operand_aliasing={{0}: (8, {}), {1}: (9, {})} | custom-call | flops 1 | bytes 1 | tf_op jit(solution)/shard_map/project/pallas_call | solution.py:102
  102.2 9.9 %attend.1 = bf16[768,1024]{1,0:T(8,128)(2,1)} custom-call(s32[24]{0:T(128)} %get-tuple-element.217.slots, s32[12]{0:T(128)} %convert_reduce_fusion.counts, bf16[768,1024]{1,0:T(8,128)(2,1)} %query_ref.1, bf16[28,128,1024]{2,1,0:T(8,128)(2,1)} %get-tuple-element.218.refs_0_.refs_1_.refs_2_.refs_3_.refs_4_.refs_5_, ...), custom_call_target="tpu_custom_call" | custom-call | flops 1 | bytes 1 | tf_op jit(solution)/shard_map/attend/pallas_call | solution.py:178
  (94 shorter events, 23.8 us)
Async XLA Ops:
  2.2 7.4 %collective-permute-start.11 = (s32[24]{0:T(128)S(1)}, s32[24]{0:T(128)S(1)}, u32[]{:S(2)}, u32[]{:S(2)}) collective-permute-start(s32[24]{0:T(128)S(1)} %reshape.130), channel_id=1, source_target_pairs={{0,12},{4,8},{8,4},{12,0},{1,13},{5,9},{9,5},{13,1},{2,14},{6,10},... | collective-permute-start | bytes 296 | tf_op jit(solution)/shard_map/ppermute | solution.py:381
  7.3 4.4 %collective-permute-start.10 = (s32[24]{0:T(128)S(1)}, s32[24]{0:T(128)S(1)}, u32[]{:S(2)}, u32[]{:S(2)}) collective-permute-start(s32[24]{0:T(128)S(1)} %reshape.130), channel_id=1, source_target_pairs={{0,8},{4,12},{8,0},{12,4},{1,9},{5,13},{9,1},{13,5},{2,10},{6,14},... | collective-permute-start | bytes 296 | tf_op jit(solution)/shard_map/ppermute | solution.py:381
  7.9 21.0 %collective-permute-start.17 = (f32[1,256]{1,0:T(1,128)}, f32[1,256]{1,0:T(1,128)S(1)}, u32[]{:S(2)}, u32[]{:S(2)}) collective-permute-start(f32[1,256]{1,0:T(1,128)} %bitcast.39), channel_id=1, source_target_pairs={{0,2},{2,0},{1,3},{3,1},{4,6},{6,4},{5,7},{7,5},{8,10},{10,8},{9,1... | collective-permute-start | bytes 3080 | tf_op jit(solution)/shard_map/ppermute | solution.py:41
  9.6 21.2 %collective-permute-start.16 = (f32[1,256]{1,0:T(1,128)}, f32[1,256]{1,0:T(1,128)S(1)}, u32[]{:S(2)}, u32[]{:S(2)}) collective-permute-start(f32[1,256]{1,0:T(1,128)} %bitcast.40), channel_id=1, source_target_pairs={{0,1},{1,0},{2,3},{3,2},{4,5},{5,4},{6,7},{7,6},{8,9},{9,8},{10,11... | collective-permute-start | bytes 3080 | tf_op jit(solution)/shard_map/ppermute | solution.py:41
  9.6 16.5 %collective-permute-start.13 = (bf16[8,128,256]{2,1,0:T(8,128)(2,1)S(1)}, bf16[8,128,256]{2,1,0:T(8,128)(2,1)S(1)}, u32[]{:S(2)}, u32[]{:S(2)}) collective-permute-start(bf16[8,128,256]{2,1,0:T(8,128)(2,1)S(1)} %get-tuple-element.138), channel_id=1, source_target_pairs={{0,4},{4,8},{8,12},{12,0},{1,5},{5,9},{9,13},{13,1},{2,6},{6,10},{... | collective-permute-start | bytes 1572872 | tf_op jit(solution)/shard_map/ppermute | solution.py:349
  13.3 24.0 %collective-permute-start.14 = (bf16[8,128,256]{2,1,0:T(8,128)(2,1)S(1)}, bf16[8,128,256]{2,1,0:T(8,128)(2,1)S(1)}, u32[]{:S(2)}, u32[]{:S(2)}) collective-permute-start(bf16[8,128,256]{2,1,0:T(8,128)(2,1)S(1)} %get-tuple-element.139), channel_id=1, source_target_pairs={{0,4},{4,8},{8,12},{12,0},{1,5},{5,9},{9,13},{13,1},{2,6},{6,10},{... | collective-permute-start | bytes 1572872 | tf_op jit(solution)/shard_map/ppermute | solution.py:349
  28.7 8.6 %collective-permute-start.15 = (bf16[4,128,256]{2,1,0:T(8,128)(2,1)S(1)}, bf16[4,128,256]{2,1,0:T(8,128)(2,1)S(1)}, u32[]{:S(2)}, u32[]{:S(2)}) collective-permute-start(bf16[4,128,256]{2,1,0:T(8,128)(2,1)S(1)} %get-tuple-element.174.refs_0_), channel_id=1, source_target_pairs={{0,1},{1,0},{2,3},{3,2},{4,5},{5,4},{6,7},{7,6},{8,9},{9,8},{10,11... | collective-permute-start | bytes 786440 | tf_op jit(solution)/shard_map/ppermute | solution.py:41
  31.5 11.1 %collective-permute-start.20 = (bf16[4,128,256]{2,1,0:T(8,128)(2,1)S(1)}, bf16[4,128,256]{2,1,0:T(8,128)(2,1)S(1)}, u32[]{:S(2)}, u32[]{:S(2)}) collective-permute-start(bf16[4,128,256]{2,1,0:T(8,128)(2,1)S(1)} %get-tuple-element.174.refs_0_), channel_id=1, source_target_pairs={{0,2},{2,0},{1,3},{3,1},{4,6},{6,4},{5,7},{7,5},{8,10},{10,8},{9,1... | collective-permute-start | bytes 786440 | tf_op jit(solution)/shard_map/ppermute | solution.py:41
  32.5 10.1 %collective-permute-start.19 = (bf16[4,128,256]{2,1,0:T(8,128)(2,1)S(1)}, bf16[4,128,256]{2,1,0:T(8,128)(2,1)S(1)}, u32[]{:S(2)}, u32[]{:S(2)}) collective-permute-start(bf16[4,128,256]{2,1,0:T(8,128)(2,1)S(1)} %get-tuple-element.143), channel_id=1, source_target_pairs={{0,4},{4,8},{8,12},{12,0},{1,5},{5,9},{9,13},{13,1},{2,6},{6,10},{... | collective-permute-start | bytes 786440 | tf_op jit(solution)/shard_map/ppermute | solution.py:349
  40.3 11.2 %collective-permute-start.23 = (bf16[4,128,256]{2,1,0:T(8,128)(2,1)S(1)}, bf16[4,128,256]{2,1,0:T(8,128)(2,1)S(1)}, u32[]{:S(2)}, u32[]{:S(2)}) collective-permute-start(bf16[4,128,256]{2,1,0:T(8,128)(2,1)S(1)} %get-tuple-element.178.refs_4_), channel_id=1, source_target_pairs={{0,2},{2,0},{1,3},{3,1},{4,6},{6,4},{5,7},{7,5},{8,10},{10,8},{9,1... | collective-permute-start | bytes 786440 | tf_op jit(solution)/shard_map/ppermute | solution.py:41
  40.6 10.9 %collective-permute-start.22 = (bf16[4,128,256]{2,1,0:T(8,128)(2,1)S(1)}, bf16[4,128,256]{2,1,0:T(8,128)(2,1)S(1)}, u32[]{:S(2)}, u32[]{:S(2)}) collective-permute-start(bf16[4,128,256]{2,1,0:T(8,128)(2,1)S(1)} %get-tuple-element.149), channel_id=1, source_target_pairs={{0,4},{4,8},{8,12},{12,0},{1,5},{5,9},{9,13},{13,1},{2,6},{6,10},{... | collective-permute-start | bytes 786440 | tf_op jit(solution)/shard_map/ppermute | solution.py:349
  44.6 7.0 %collective-permute-start.24 = (bf16[4,128,256]{2,1,0:T(8,128)(2,1)S(1)}, bf16[4,128,256]{2,1,0:T(8,128)(2,1)S(1)}, u32[]{:S(2)}, u32[]{:S(2)}) collective-permute-start(bf16[4,128,256]{2,1,0:T(8,128)(2,1)S(1)} %get-tuple-element.194.refs_0_), channel_id=1, source_target_pairs={{0,1},{1,0},{2,3},{3,2},{4,5},{5,4},{6,7},{7,6},{8,9},{9,8},{10,11... | collective-permute-start | bytes 786440 | tf_op jit(solution)/shard_map/ppermute | solution.py:41
  44.7 13.5 %collective-permute-start.27 = (bf16[4,128,256]{2,1,0:T(8,128)(2,1)S(1)}, bf16[4,128,256]{2,1,0:T(8,128)(2,1)S(1)}, u32[]{:S(2)}, u32[]{:S(2)}) collective-permute-start(bf16[4,128,256]{2,1,0:T(8,128)(2,1)S(1)} %get-tuple-element.194.refs_0_), channel_id=1, source_target_pairs={{0,2},{2,0},{1,3},{3,1},{4,6},{6,4},{5,7},{7,5},{8,10},{10,8},{9,1... | collective-permute-start | bytes 786440 | tf_op jit(solution)/shard_map/ppermute | solution.py:41
  45.4 11.1 %collective-permute-start.26 = (bf16[4,128,256]{2,1,0:T(8,128)(2,1)S(1)}, bf16[4,128,256]{2,1,0:T(8,128)(2,1)S(1)}, u32[]{:S(2)}, u32[]{:S(2)}) collective-permute-start(bf16[4,128,256]{2,1,0:T(8,128)(2,1)S(1)} %get-tuple-element.157), channel_id=1, source_target_pairs={{0,4},{4,8},{8,12},{12,0},{1,5},{5,9},{9,13},{13,1},{2,6},{6,10},{... | collective-permute-start | bytes 786440 | tf_op jit(solution)/shard_map/ppermute | solution.py:349
  53.5 4.7 %collective-permute-start.28 = (bf16[4,128,256]{2,1,0:T(8,128)(2,1)S(1)}, bf16[4,128,256]{2,1,0:T(8,128)(2,1)S(1)}, u32[]{:S(2)}, u32[]{:S(2)}) collective-permute-start(bf16[4,128,256]{2,1,0:T(8,128)(2,1)S(1)} %get-tuple-element.198.refs_4_), channel_id=1, source_target_pairs={{0,1},{1,0},{2,3},{3,2},{4,5},{5,4},{6,7},{7,6},{8,9},{9,8},{10,11... | collective-permute-start | bytes 786440 | tf_op jit(solution)/shard_map/ppermute | solution.py:41
  53.6 6.5 %collective-permute-start.31 = (bf16[4,128,256]{2,1,0:T(8,128)(2,1)S(1)}, bf16[4,128,256]{2,1,0:T(8,128)(2,1)S(1)}, u32[]{:S(2)}, u32[]{:S(2)}) collective-permute-start(bf16[4,128,256]{2,1,0:T(8,128)(2,1)S(1)} %collective-permute-done.20.refs_2_), channel_id=1, source_target_pairs={{0,1},{1,0},{2,3},{3,2},{4,5},{5,4},{6,7},{7,6},{8,9},{9,8},{10,11... | collective-permute-start | bytes 786440 | tf_op jit(solution)/shard_map/ppermute | solution.py:41
  54.1 6.1 %collective-permute-start.32 = (bf16[4,128,256]{2,1,0:T(8,128)(2,1)S(1)}, bf16[4,128,256]{2,1,0:T(8,128)(2,1)S(1)}, u32[]{:S(2)}, u32[]{:S(2)}) collective-permute-start(bf16[4,128,256]{2,1,0:T(8,128)(2,1)S(1)} %collective-permute-done.23.refs_6_), channel_id=1, source_target_pairs={{0,1},{1,0},{2,3},{3,2},{4,5},{5,4},{6,7},{7,6},{8,9},{9,8},{10,11... | collective-permute-start | bytes 786440 | tf_op jit(solution)/shard_map/ppermute | solution.py:41
  56.5 8.5 %collective-permute-start.33 = (bf16[4,128,256]{2,1,0:T(8,128)(2,1)S(1)}, bf16[4,128,256]{2,1,0:T(8,128)(2,1)S(1)}, u32[]{:S(2)}, u32[]{:S(2)}) collective-permute-start(bf16[4,128,256]{2,1,0:T(8,128)(2,1)S(1)} %get-tuple-element.198.refs_4_), channel_id=1, source_target_pairs={{0,2},{2,0},{1,3},{3,1},{4,6},{6,4},{5,7},{7,5},{8,10},{10,8},{9,1... | collective-permute-start | bytes 786440 | tf_op jit(solution)/shard_map/ppermute | solution.py:41
  58.2 14.0 %collective-permute-start.25 = (bf16[4,128,256]{2,1,0:T(8,128)(2,1)S(1)}, bf16[4,128,256]{2,1,0:T(8,128)(2,1)S(1)}, u32[]{:S(2)}, u32[]{:S(2)}) collective-permute-start(bf16[4,128,256]{2,1,0:T(8,128)(2,1)S(1)} %get-tuple-element.156), channel_id=1, source_target_pairs={{0,4},{4,8},{8,12},{12,0},{1,5},{5,9},{9,13},{13,1},{2,6},{6,10},{... | collective-permute-start | bytes 786440 | tf_op jit(solution)/shard_map/ppermute | solution.py:349
  60.1 12.8 %collective-permute-start.29 = (bf16[4,128,256]{2,1,0:T(8,128)(2,1)S(1)}, bf16[4,128,256]{2,1,0:T(8,128)(2,1)S(1)}, u32[]{:S(2)}, u32[]{:S(2)}) collective-permute-start(bf16[4,128,256]{2,1,0:T(8,128)(2,1)S(1)} %get-tuple-element.165), channel_id=1, source_target_pairs={{0,4},{4,8},{8,12},{12,0},{1,5},{5,9},{9,13},{13,1},{2,6},{6,10},{... | collective-permute-start | bytes 786440 | tf_op jit(solution)/shard_map/ppermute | solution.py:349
  60.1 12.8 %collective-permute-start.30 = (bf16[4,128,256]{2,1,0:T(8,128)(2,1)S(1)}, bf16[4,128,256]{2,1,0:T(8,128)(2,1)S(1)}, u32[]{:S(2)}, u32[]{:S(2)}) collective-permute-start(bf16[4,128,256]{2,1,0:T(8,128)(2,1)S(1)} %get-tuple-element.202.refs_8_), channel_id=1, source_target_pairs={{0,1},{1,0},{2,3},{3,2},{4,5},{5,4},{6,7},{7,6},{8,9},{9,8},{10,11... | collective-permute-start | bytes 786440 | tf_op jit(solution)/shard_map/ppermute | solution.py:41
  60.2 17.3 %collective-permute-start.38 = (bf16[4,128,256]{2,1,0:T(8,128)(2,1)S(1)}, bf16[4,128,256]{2,1,0:T(8,128)(2,1)S(1)}, u32[]{:S(2)}, u32[]{:S(2)}) collective-permute-start(bf16[4,128,256]{2,1,0:T(8,128)(2,1)S(1)} %get-tuple-element.202.refs_8_), channel_id=1, source_target_pairs={{0,2},{2,0},{1,3},{3,1},{4,6},{6,4},{5,7},{7,5},{8,10},{10,8},{9,1... | collective-permute-start | bytes 786440 | tf_op jit(solution)/shard_map/ppermute | solution.py:41
  75.1 12.3 %collective-permute-start.35 = (bf16[8,128,256]{2,1,0:T(8,128)(2,1)S(1)}, bf16[8,128,256]{2,1,0:T(8,128)(2,1)S(1)}, u32[]{:S(2)}, u32[]{:S(2)}) collective-permute-start(bf16[8,128,256]{2,1,0:T(8,128)(2,1)S(1)} %pack.11.refs_0_), channel_id=1, source_target_pairs={{0,2},{2,0},{1,3},{3,1},{4,6},{6,4},{5,7},{7,5},{8,10},{10,8},{9,1... | collective-permute-start | bytes 1572872 | tf_op jit(solution)/shard_map/ppermute | solution.py:41
  77.0 10.4 %collective-permute-start.34 = (bf16[8,128,256]{2,1,0:T(8,128)(2,1)S(1)}, bf16[8,128,256]{2,1,0:T(8,128)(2,1)S(1)}, u32[]{:S(2)}, u32[]{:S(2)}) collective-permute-start(bf16[8,128,256]{2,1,0:T(8,128)(2,1)S(1)} %pack.11.refs_0_), channel_id=1, source_target_pairs={{0,1},{1,0},{2,3},{3,2},{4,5},{5,4},{6,7},{7,6},{8,9},{9,8},{10,11... | collective-permute-start | bytes 1572872 | tf_op jit(solution)/shard_map/ppermute | solution.py:41
  (15 other events, 117.3 us)

commit v2 on v1

--- a/solution.py
+++ b/solution.py
@@ -25,6 +25,7 @@
 CAP = 4
 GROUP = 2
 SWEEPS = ROUNDS + 1
+LARGE = 176
 SWEPT = (CAP,) * ROUNDS + (2 * CAP,)
 LANES = 128
 
@@ -47,7 +48,7 @@
     columns = key_weight.shape[1]
     each = count // group
     rows = group * tokens
-    groups = total // group
+    groups = (marks.shape[0] - pieces) // 2
 
     def kernel(marks_ref, gain_ref, *refs):
         arrays, weights = refs[: len(rounds) * pieces], refs[len(rounds) * pieces : len(rounds) * pieces + 2]
@@ -422,7 +423,7 @@
             pieces[number - 1].append(swapped(pieces[number - 1][2], "rep"))
         if number == SWEEPS - 2:
             ripe, pieces[number - 1][2] = lax.optimization_barrier((pieces[:2], pieces[number - 1][2]))
-            held = project(marks, gain, ripe, key_weight, value_weight, GROUP, room)
+            held = project(marks, gain, ripe, key_weight, value_weight, GROUP, LARGE)
         if number + 1 < SWEEPS:
             across = [parts[2] for parts in pieces[:number]] if number + 2 < SWEEPS else []
             came = slice(number + 1, number + 2 if number + 2 < SWEEPS else None)
@@ -432,16 +433,16 @@
             for parts, arrived in zip(pieces, across):
                 parts[2] = arrived
     ripe, _ = lax.optimization_barrier((pieces[2:-1], mine))
-    held = project(marks, gain, ripe, key_weight, value_weight, GROUP, room, 2 * CAP // GROUP, held)
+    held = project(marks, gain, ripe, key_weight, value_weight, GROUP, LARGE, 2 * CAP // GROUP, held)
     late, held = lax.optimization_barrier((pieces[-1], held))
     late = [*late, swapped(late[2], "rep")]
     done = (SWEEPS - 1) * CAP // GROUP
-    keys, values = project(marks, gain, [late], key_weight, value_weight, GROUP, room, done, held)
+    keys, values = project(marks, gain, [late], key_weight, value_weight, GROUP, LARGE, done, held)
 
     def whole(state):
         mine = fetch_all(store, asked >> 4, asked & (ENTRIES_EACH - 1))
         marks = every_group(places, room // 4)
-        keys, values = project(marks, gain, [four_pieces(mine)], key_weight, value_weight, 4, room)
+        keys, values = project(marks, gain, [four_pieces(mine)], key_weight, value_weight, 4, LARGE)
         return jnp.zeros_like(state[0]), jnp.arange(total, dtype=jnp.int32), keys, values
 
     state = lax.while_loop(lambda state: state[0] > 0, whole, (missing, slots, keys, values))

time: 112 us -> 109 us (0.973)
  local copies, waits for them, and re-layouts: 12.3 us -> 7.11 us
  Pallas kernels: 45.9 us -> 47.9 us
    unnamed x14 -> x10, local copies, waits for them, and re-layouts: 6.55 us -> 1.39 us
    pallas_call x3, Pallas kernels: 21.4 us -> 23.7 us  [project(): pl.pallas_call(kernel, out_shape=(out, out), grid_spec=pltpu.PrefetchScal...]
  transfers between devices with their start and end apart: 32 -> 32, of which waited for: 13 -> 12; matrix products, arithmetic and copies ran while one was open for 6% -> 6% of each run, Pallas kernels for 26% -> 27%
where the time goes in v2:
time: 109 us
  Pallas kernels  47.9 us (44%)
  waiting for transfers between devices  29.8 us (27%)
  starting transfers between devices  20.4 us (19%)
  local copies, waits for them, and re-layouts  7.11 us (7%)
  other arithmetic  2.66 us (2%)
    pallas_call x3, Pallas kernels, project(): pl.pallas_call(kernel, out_shape=(out, out), grid_spec=pltpu.PrefetchScal...  23.7 us
    ppermute x7, waiting for transfers between devices, onward(): lax.ppermute(value, 'seq', [(chip, (chip + 1) % size) for chip in range(s...  20.6 us
    ppermute x22, starting transfers between devices, swapped(): return lax.ppermute(value, axis, [(0, 1), (1, 0)])  12.4 us
    pallas_call x6, Pallas kernels, pack(): pl.pallas_call(kernel, out_shape=tuple((jax.ShapeDtypeStruct((cap,) + poo...  12 us
    pallas_call x1, Pallas kernels, attend(): pl.pallas_call(attend_kernel, out_shape=jax.ShapeDtypeStruct(queries.shap...  9.69 us
    ppermute x22, waiting for transfers between devices, swapped(): return lax.ppermute(value, axis, [(0, 1), (1, 0)])  8.36 us
    ppermute x3, starting transfers between devices, exchanged_table(): lax.ppermute(codes, 'seq', [(chip, chip ^ offset) for chip in range(CHIPS)])  5.76 us
    pallas_call x1, Pallas kernels, make_plan(): pl.pallas_call(plan_kernel, out_shape=jax.ShapeDtypeStruct((8, LANES), jn...  2.53 us
  transfers between devices with their start and end apart: 32, of which 12 were waited for; matrix products, arithmetic and copies ran while one was open for 6% of the time, Pallas kernels for 27%

profile of v2, /device:TPU:0, one launch (start us, length us, event | category | flops | bytes accessed | tf_op | source)
XLA Modules:
  0.0 109.0 jit_solution(6289177510604246615)
XLA Ops:
  0.9 1.3 %fusion.7 = (bf16[8,128,256]{2,1,0:T(8,128)(2,1)S(1)}, bf16[8,128,256]{2,1,0:T(8,128)(2,1)S(1)}) fusion(bf16[16,128,256]{2,1,0:T(8,128)(2,1)} %refs_0_.11), kind=kLoop, calls=%fused_computation.38 | loop fusion | bytes 2097152 | tf_op jit(solution)/shard_map/slice | solution.py:394
  2.2 5.1 %collective-permute-start.11 = (s32[24]{0:T(128)S(1)}, s32[24]{0:T(128)S(1)}, u32[]{:S(2)}, u32[]{:S(2)}) collective-permute-start(s32[24]{0:T(128)S(1)} %reshape.130), channel_id=1, source_target_pairs={{0,12},{4,8},{8,4},{12,0},{1,13},{5,9},{9,5},{13,1},{2,14},{6,10},... | collective-permute-start | bytes 296 | tf_op jit(solution)/shard_map/ppermute | solution.py:382
  7.9 1.6 %collective-permute-start.17 = (f32[1,256]{1,0:T(1,128)}, f32[1,256]{1,0:T(1,128)S(1)}, u32[]{:S(2)}, u32[]{:S(2)}) collective-permute-start(f32[1,256]{1,0:T(1,128)} %bitcast.39), channel_id=1, source_target_pairs={{0,2},{2,0},{1,3},{3,1},{4,6},{6,4},{5,7},{7,5},{8,10},{10,8},{9,1... | collective-permute-start | bytes 3080 | tf_op jit(solution)/shard_map/ppermute | solution.py:42
  11.7 1.6 %collective-permute-start.12 = (s32[4,24]{1,0:T(4,128)S(1)}, s32[4,24]{1,0:T(4,128)S(1)}, u32[]{:S(2)}, u32[]{:S(2)}) collective-permute-start(s32[4,24]{1,0:T(4,128)S(1)} %pad_add_fusion.2), channel_id=1, source_target_pairs={{0,16},{16,0},{1,17},{17,1},{2,18},{18,2},{3,19},{19,3},{4,20},{20... | collective-permute-start | bytes 1160 | tf_op jit(solution)/shard_map/ppermute | solution.py:42
  13.9 1.5 %collective-permute-done.12 = s32[4,24]{1,0:T(4,128)S(1)} collective-permute-done((s32[4,24]{1,0:T(4,128)S(1)}, s32[4,24]{1,0:T(4,128)S(1)}, u32[]{:S(2)}, u32[]{:S(2)}) %collective-permute-start.12) | collective-permute-done | bytes 416 | tf_op jit(solution)/shard_map/ppermute | solution.py:42
  16.5 2.5 %plan.1 = s32[8,128]{1,0:T(8,128)} custom-call(s32[1]{0:T(128)} %bitcast.2.place, s32[192]{0:T(256)} %reshape.131.table), custom_call_target="tpu_custom_call" | custom-call | tf_op jit(solution)/shard_map/plan/pallas_call | solution.py:286
  20.8 5.3 %collective-permute-done.13.refs_1_ = bf16[8,128,256]{2,1,0:T(8,128)(2,1)S(1)} collective-permute-done((bf16[8,128,256]{2,1,0:T(8,128)(2,1)S(1)}, bf16[8,128,256]{2,1,0:T(8,128)(2,1)S(1)}, u32[]{:S(2)}, u32[]{:S(2)}) %collective-permute-start.13) | collective-permute-done | bytes 524320 | tf_op jit(solution)/shard_map/ppermute | solution.py:350
  26.8 1.9 %pack.6 = (bf16[4,128,256]{2,1,0:T(8,128)(2,1)S(1)}, bf16[4,128,256]{2,1,0:T(8,128)(2,1)S(1)}) custom-call(s32[1024]{0:T(1024)S(1)} %bitcast.23, bf16[16,128,256]{2,1,0:T(8,128)(2,1)} %refs_0_.11, bf16[8,128,256]{2,1,0:T(8,128)(2,1)S(1)} %collective-permute-done.13.refs_1_), custom_call_target="tpu_custom_call" | custom-call | flops 1 | bytes 1 | tf_op jit(solution)/shard_map/pack/pallas_call | solution.py:314
  32.4 4.9 %collective-permute-done.14.refs_2_ = bf16[8,128,256]{2,1,0:T(8,128)(2,1)S(1)} collective-permute-done((bf16[8,128,256]{2,1,0:T(8,128)(2,1)S(1)}, bf16[8,128,256]{2,1,0:T(8,128)(2,1)S(1)}, u32[]{:S(2)}, u32[]{:S(2)}) %collective-permute-start.14) | collective-permute-done | bytes 524320 | tf_op jit(solution)/shard_map/ppermute | solution.py:350
  38.0 2.3 %pack.7 = (bf16[4,128,256]{2,1,0:T(8,128)(2,1)S(1)}, bf16[4,128,256]{2,1,0:T(8,128)(2,1)S(1)}) custom-call(s32[1024]{0:T(1024)S(1)} %bitcast.24, bf16[16,128,256]{2,1,0:T(8,128)(2,1)} %refs_0_.11, bf16[8,128,256]{2,1,0:T(8,128)(2,1)S(1)} %collective-permute-done.13.refs_1_, bf16[8,128,256]{2,1,0:T(8,128)(2,1)S(1)} %collective-permute-done.14.refs_2_), custom_call_target="tpu_custom_call" | custom-call | flops 1 | bytes 1 | tf_op jit(solution)/shard_map/pack/pallas_call | solution.py:314
  40.6 2.0 %collective-permute-done.19.refs_3_ = bf16[4,128,256]{2,1,0:T(8,128)(2,1)S(1)} collective-permute-done((bf16[4,128,256]{2,1,0:T(8,128)(2,1)S(1)}, bf16[4,128,256]{2,1,0:T(8,128)(2,1)S(1)}, u32[]{:S(2)}, u32[]{:S(2)}) %collective-permute-start.19) | collective-permute-done | bytes 262176 | tf_op jit(solution)/shard_map/ppermute | solution.py:350
  42.6 1.8 %pack.8 = (bf16[4,128,256]{2,1,0:T(8,128)(2,1)S(1)}, bf16[4,128,256]{2,1,0:T(8,128)(2,1)S(1)}) custom-call(s32[1024]{0:T(1024)S(1)} %bitcast.25, bf16[16,128,256]{2,1,0:T(8,128)(2,1)} %refs_0_.11, bf16[8,128,256]{2,1,0:T(8,128)(2,1)S(1)} %collective-permute-done.13.refs_1_, bf16[8,128,256]{2,1,0:T(8,128)(2,1)S(1)} %collective-permute-done.14.refs_2_, ...), custom_call_target="tpu_custom_call" | custom-call | flops 1 | bytes 1 | tf_op jit(solution)/shard_map/pack/pallas_call | solution.py:314
  45.5 6.1 %collective-permute-done.22.refs_4_ = bf16[4,128,256]{2,1,0:T(8,128)(2,1)S(1)} collective-permute-done((bf16[4,128,256]{2,1,0:T(8,128)(2,1)S(1)}, bf16[4,128,256]{2,1,0:T(8,128)(2,1)S(1)}, u32[]{:S(2)}, u32[]{:S(2)}) %collective-permute-start.22) | collective-permute-done | bytes 262176 | tf_op jit(solution)/shard_map/ppermute | solution.py:350
  51.6 1.9 %pack.9 = (bf16[4,128,256]{2,1,0:T(8,128)(2,1)S(1)}, bf16[4,128,256]{2,1,0:T(8,128)(2,1)S(1)}) custom-call(s32[1024]{0:T(1024)S(1)} %bitcast.26, bf16[16,128,256]{2,1,0:T(8,128)(2,1)} %refs_0_.11, bf16[8,128,256]{2,1,0:T(8,128)(2,1)S(1)} %collective-permute-done.13.refs_1_, bf16[8,128,256]{2,1,0:T(8,128)(2,1)S(1)} %collective-permute-done.14.refs_2_, ...), custom_call_target="tpu_custom_call" | custom-call | flops 1 | bytes 1 | tf_op jit(solution)/shard_map/pack/pallas_call | solution.py:314
  54.2 2.3 %collective-permute-done.26.refs_5_ = bf16[4,128,256]{2,1,0:T(8,128)(2,1)S(1)} collective-permute-done((bf16[4,128,256]{2,1,0:T(8,128)(2,1)S(1)}, bf16[4,128,256]{2,1,0:T(8,128)(2,1)S(1)}, u32[]{:S(2)}, u32[]{:S(2)}) %collective-permute-start.26) | collective-permute-done | bytes 262176 | tf_op jit(solution)/shard_map/ppermute | solution.py:350
  56.5 1.8 %collective-permute-start.33 = (bf16[4,128,256]{2,1,0:T(8,128)(2,1)S(1)}, bf16[4,128,256]{2,1,0:T(8,128)(2,1)S(1)}, u32[]{:S(2)}, u32[]{:S(2)}) collective-permute-start(bf16[4,128,256]{2,1,0:T(8,128)(2,1)S(1)} %get-tuple-element.198.refs_4_), channel_id=1, source_target_pairs={{0,2},{2,0},{1,3},{3,1},{4,6},{6,4},{5,7},{7,5},{8,10},{10,8},{9,1... | collective-permute-start | bytes 786440 | tf_op jit(solution)/shard_map/ppermute | solution.py:42
  58.2 1.9 %pack.10 = (bf16[4,128,256]{2,1,0:T(8,128)(2,1)S(1)}, bf16[4,128,256]{2,1,0:T(8,128)(2,1)S(1)}) custom-call(s32[1024]{0:T(1024)S(1)} %bitcast.27, bf16[16,128,256]{2,1,0:T(8,128)(2,1)} %refs_0_.11, bf16[8,128,256]{2,1,0:T(8,128)(2,1)S(1)} %collective-permute-done.13.refs_1_, bf16[8,128,256]{2,1,0:T(8,128)(2,1)S(1)} %collective-permute-done.14.refs_2_, ...), custom_call_target="tpu_custom_call" | custom-call | flops 1 | bytes 1 | tf_op jit(solution)/shard_map/pack/pallas_call | solution.py:314
  60.7 4.3 %collective-permute-done.33.refs_6_ = bf16[4,128,256]{2,1,0:T(8,128)(2,1)S(1)} collective-permute-done((bf16[4,128,256]{2,1,0:T(8,128)(2,1)S(1)}, bf16[4,128,256]{2,1,0:T(8,128)(2,1)S(1)}, u32[]{:S(2)}, u32[]{:S(2)}) %collective-permute-start.33) | collective-permute-done | bytes 262176 | tf_op jit(solution)/shard_map/ppermute | solution.py:42
  65.0 8.4 %project.5 = (bf16[176,128,1024]{2,1,0:T(8,128)(2,1)}, bf16[176,128,1024]{2,1,0:T(8,128)(2,1)}) custom-call(s32[32]{0:T(128)S(1)} %concatenate.23.marks_ref, f32[1,1024]{1,0:T(1,128)S(1)} %pad_maximum_fusion.gain_ref, bf16[4,128,256]{2,1,0:T(8,128)(2,1)S(1)} %get-tuple-element.174.refs_0_, bf16[4,128,256]{2,1,0:T(8,128)(2,1)S(1)} %collective-permute-done.15.refs_1_, ...), custom_call_target="tpu_custom_call" | custom-call | flops 1 | bytes 1 | tf_op jit(solution)/shard_map/project/pallas_call | solution.py:103
  73.4 2.1 %pack.11.refs_0_ = bf16[8,128,256]{2,1,0:T(8,128)(2,1)S(1)} custom-call(s32[1024]{0:T(1024)S(1)} %bitcast.28, bf16[16,128,256]{2,1,0:T(8,128)(2,1)} %refs_0_.11, bf16[8,128,256]{2,1,0:T(8,128)(2,1)S(1)} %collective-permute-done.13.refs_1_, bf16[8,128,256]{2,1,0:T(8,128)(2,1)S(1)} %collective-permute-done.14.refs_2_, ...), custom_call_target="tpu_custom_call" | custom-call | flops 1 | bytes 1 | tf_op jit(solution)/shard_map/pack/pallas_call | solution.py:314
  75.5 2.5 %collective-permute-start.35 = (bf16[8,128,256]{2,1,0:T(8,128)(2,1)S(1)}, bf16[8,128,256]{2,1,0:T(8,128)(2,1)S(1)}, u32[]{:S(2)}, u32[]{:S(2)}) collective-permute-start(bf16[8,128,256]{2,1,0:T(8,128)(2,1)S(1)} %pack.11.refs_0_), channel_id=1, source_target_pairs={{0,2},{2,0},{1,3},{3,1},{4,6},{6,4},{5,7},{7,5},{8,10},{10,8},{9,1... | collective-permute-start | bytes 1572872 | tf_op jit(solution)/shard_map/ppermute | solution.py:42
  81.1 7.1 %project.6 = (bf16[176,128,1024]{2,1,0:T(8,128)(2,1)}, bf16[176,128,1024]{2,1,0:T(8,128)(2,1)}) custom-call(s32[32]{0:T(128)S(1)} %concatenate.23.marks_ref, f32[1,1024]{1,0:T(1,128)S(1)} %pad_maximum_fusion.gain_ref, bf16[4,128,256]{2,1,0:T(8,128)(2,1)S(1)} %get-tuple-element.194.refs_0_, ...), custom_call_target="tpu_custom_call", output_to_operand_aliasing={{0}: (16, {}), {1}: (17, {})} | custom-call | flops 1 | bytes 1 | tf_op jit(solution)/shard_map/project/pallas_call | solution.py:103
  90.2 8.3 %project.7 = (bf16[176,128,1024]{2,1,0:T(8,128)(2,1)}, bf16[176,128,1024]{2,1,0:T(8,128)(2,1)}) custom-call(s32[32]{0:T(128)S(1)} %concatenate.23.marks_ref, f32[1,1024]{1,0:T(1,128)S(1)} %pad_maximum_fusion.gain_ref, bf16[8,128,256]{2,1,0:T(8,128)(2,1)S(1)} %pack.11.refs_0_, ...), custom_call_target="tpu_custom_call", output_to_operand_aliasing={{0}: (8, {}), {1}: (9, {})} | custom-call | flops 1 | bytes 1 | tf_op jit(solution)/shard_map/project/pallas_call | solution.py:103
  99.4 9.7 %attend.1 = bf16[768,1024]{1,0:T(8,128)(2,1)} custom-call(s32[24]{0:T(128)} %get-tuple-element.217.slots, s32[12]{0:T(128)} %convert_reduce_fusion.counts, bf16[768,1024]{1,0:T(8,128)(2,1)} %query_ref.1, bf16[176,128,1024]{2,1,0:T(8,128)(2,1)} %get-tuple-element.218.refs_0_.refs_1_.refs_2_.refs_3_.refs_4_.refs_5_, ...), custom_call_target="tpu_custom_call" | custom-call | flops 1 | bytes 1 | tf_op jit(solution)/shard_map/attend/pallas_call | solution.py:179
  (90 shorter events, 20.6 us)
Async XLA Ops:
  2.2 7.4 %collective-permute-start.11 = (s32[24]{0:T(128)S(1)}, s32[24]{0:T(128)S(1)}, u32[]{:S(2)}, u32[]{:S(2)}) collective-permute-start(s32[24]{0:T(128)S(1)} %reshape.130), channel_id=1, source_target_pairs={{0,12},{4,8},{8,4},{12,0},{1,13},{5,9},{9,5},{13,1},{2,14},{6,10},... | collective-permute-start | bytes 296 | tf_op jit(solution)/shard_map/ppermute | solution.py:382
  7.3 4.4 %collective-permute-start.10 = (s32[24]{0:T(128)S(1)}, s32[24]{0:T(128)S(1)}, u32[]{:S(2)}, u32[]{:S(2)}) collective-permute-start(s32[24]{0:T(128)S(1)} %reshape.130), channel_id=1, source_target_pairs={{0,8},{4,12},{8,0},{12,4},{1,9},{5,13},{9,1},{13,5},{2,10},{6,14},... | collective-permute-start | bytes 296 | tf_op jit(solution)/shard_map/ppermute | solution.py:382
  7.9 21.0 %collective-permute-start.17 = (f32[1,256]{1,0:T(1,128)}, f32[1,256]{1,0:T(1,128)S(1)}, u32[]{:S(2)}, u32[]{:S(2)}) collective-permute-start(f32[1,256]{1,0:T(1,128)} %bitcast.39), channel_id=1, source_target_pairs={{0,2},{2,0},{1,3},{3,1},{4,6},{6,4},{5,7},{7,5},{8,10},{10,8},{9,1... | collective-permute-start | bytes 3080 | tf_op jit(solution)/shard_map/ppermute | solution.py:42
  9.6 21.2 %collective-permute-start.16 = (f32[1,256]{1,0:T(1,128)}, f32[1,256]{1,0:T(1,128)S(1)}, u32[]{:S(2)}, u32[]{:S(2)}) collective-permute-start(f32[1,256]{1,0:T(1,128)} %bitcast.40), channel_id=1, source_target_pairs={{0,1},{1,0},{2,3},{3,2},{4,5},{5,4},{6,7},{7,6},{8,9},{9,8},{10,11... | collective-permute-start | bytes 3080 | tf_op jit(solution)/shard_map/ppermute | solution.py:42
  9.6 16.5 %collective-permute-start.13 = (bf16[8,128,256]{2,1,0:T(8,128)(2,1)S(1)}, bf16[8,128,256]{2,1,0:T(8,128)(2,1)S(1)}, u32[]{:S(2)}, u32[]{:S(2)}) collective-permute-start(bf16[8,128,256]{2,1,0:T(8,128)(2,1)S(1)} %get-tuple-element.138), channel_id=1, source_target_pairs={{0,4},{4,8},{8,12},{12,0},{1,5},{5,9},{9,13},{13,1},{2,6},{6,10},{... | collective-permute-start | bytes 1572872 | tf_op jit(solution)/shard_map/ppermute | solution.py:350
  13.3 24.0 %collective-permute-start.14 = (bf16[8,128,256]{2,1,0:T(8,128)(2,1)S(1)}, bf16[8,128,256]{2,1,0:T(8,128)(2,1)S(1)}, u32[]{:S(2)}, u32[]{:S(2)}) collective-permute-start(bf16[8,128,256]{2,1,0:T(8,128)(2,1)S(1)} %get-tuple-element.139), channel_id=1, source_target_pairs={{0,4},{4,8},{8,12},{12,0},{1,5},{5,9},{9,13},{13,1},{2,6},{6,10},{... | collective-permute-start | bytes 1572872 | tf_op jit(solution)/shard_map/ppermute | solution.py:350
  28.7 8.6 %collective-permute-start.15 = (bf16[4,128,256]{2,1,0:T(8,128)(2,1)S(1)}, bf16[4,128,256]{2,1,0:T(8,128)(2,1)S(1)}, u32[]{:S(2)}, u32[]{:S(2)}) collective-permute-start(bf16[4,128,256]{2,1,0:T(8,128)(2,1)S(1)} %get-tuple-element.174.refs_0_), channel_id=1, source_target_pairs={{0,1},{1,0},{2,3},{3,2},{4,5},{5,4},{6,7},{7,6},{8,9},{9,8},{10,11... | collective-permute-start | bytes 786440 | tf_op jit(solution)/shard_map/ppermute | solution.py:42
  31.4 11.2 %collective-permute-start.20 = (bf16[4,128,256]{2,1,0:T(8,128)(2,1)S(1)}, bf16[4,128,256]{2,1,0:T(8,128)(2,1)S(1)}, u32[]{:S(2)}, u32[]{:S(2)}) collective-permute-start(bf16[4,128,256]{2,1,0:T(8,128)(2,1)S(1)} %get-tuple-element.174.refs_0_), channel_id=1, source_target_pairs={{0,2},{2,0},{1,3},{3,1},{4,6},{6,4},{5,7},{7,5},{8,10},{10,8},{9,1... | collective-permute-start | bytes 786440 | tf_op jit(solution)/shard_map/ppermute | solution.py:42
  32.4 10.2 %collective-permute-start.19 = (bf16[4,128,256]{2,1,0:T(8,128)(2,1)S(1)}, bf16[4,128,256]{2,1,0:T(8,128)(2,1)S(1)}, u32[]{:S(2)}, u32[]{:S(2)}) collective-permute-start(bf16[4,128,256]{2,1,0:T(8,128)(2,1)S(1)} %get-tuple-element.143), channel_id=1, source_target_pairs={{0,4},{4,8},{8,12},{12,0},{1,5},{5,9},{9,13},{13,1},{2,6},{6,10},{... | collective-permute-start | bytes 786440 | tf_op jit(solution)/shard_map/ppermute | solution.py:350
  40.3 11.2 %collective-permute-start.23 = (bf16[4,128,256]{2,1,0:T(8,128)(2,1)S(1)}, bf16[4,128,256]{2,1,0:T(8,128)(2,1)S(1)}, u32[]{:S(2)}, u32[]{:S(2)}) collective-permute-start(bf16[4,128,256]{2,1,0:T(8,128)(2,1)S(1)} %get-tuple-element.178.refs_4_), channel_id=1, source_target_pairs={{0,2},{2,0},{1,3},{3,1},{4,6},{6,4},{5,7},{7,5},{8,10},{10,8},{9,1... | collective-permute-start | bytes 786440 | tf_op jit(solution)/shard_map/ppermute | solution.py:42
  40.6 10.9 %collective-permute-start.22 = (bf16[4,128,256]{2,1,0:T(8,128)(2,1)S(1)}, bf16[4,128,256]{2,1,0:T(8,128)(2,1)S(1)}, u32[]{:S(2)}, u32[]{:S(2)}) collective-permute-start(bf16[4,128,256]{2,1,0:T(8,128)(2,1)S(1)} %get-tuple-element.149), channel_id=1, source_target_pairs={{0,4},{4,8},{8,12},{12,0},{1,5},{5,9},{9,13},{13,1},{2,6},{6,10},{... | collective-permute-start | bytes 786440 | tf_op jit(solution)/shard_map/ppermute | solution.py:350
  44.4 7.1 %collective-permute-start.24 = (bf16[4,128,256]{2,1,0:T(8,128)(2,1)S(1)}, bf16[4,128,256]{2,1,0:T(8,128)(2,1)S(1)}, u32[]{:S(2)}, u32[]{:S(2)}) collective-permute-start(bf16[4,128,256]{2,1,0:T(8,128)(2,1)S(1)} %get-tuple-element.194.refs_0_), channel_id=1, source_target_pairs={{0,1},{1,0},{2,3},{3,2},{4,5},{5,4},{6,7},{7,6},{8,9},{9,8},{10,11... | collective-permute-start | bytes 786440 | tf_op jit(solution)/shard_map/ppermute | solution.py:42
  44.4 13.8 %collective-permute-start.27 = (bf16[4,128,256]{2,1,0:T(8,128)(2,1)S(1)}, bf16[4,128,256]{2,1,0:T(8,128)(2,1)S(1)}, u32[]{:S(2)}, u32[]{:S(2)}) collective-permute-start(bf16[4,128,256]{2,1,0:T(8,128)(2,1)S(1)} %get-tuple-element.194.refs_0_), channel_id=1, source_target_pairs={{0,2},{2,0},{1,3},{3,1},{4,6},{6,4},{5,7},{7,5},{8,10},{10,8},{9,1... | collective-permute-start | bytes 786440 | tf_op jit(solution)/shard_map/ppermute | solution.py:42
  45.1 11.4 %collective-permute-start.26 = (bf16[4,128,256]{2,1,0:T(8,128)(2,1)S(1)}, bf16[4,128,256]{2,1,0:T(8,128)(2,1)S(1)}, u32[]{:S(2)}, u32[]{:S(2)}) collective-permute-start(bf16[4,128,256]{2,1,0:T(8,128)(2,1)S(1)} %get-tuple-element.157), channel_id=1, source_target_pairs={{0,4},{4,8},{8,12},{12,0},{1,5},{5,9},{9,13},{13,1},{2,6},{6,10},{... | collective-permute-start | bytes 786440 | tf_op jit(solution)/shard_map/ppermute | solution.py:350
  53.5 4.7 %collective-permute-start.28 = (bf16[4,128,256]{2,1,0:T(8,128)(2,1)S(1)}, bf16[4,128,256]{2,1,0:T(8,128)(2,1)S(1)}, u32[]{:S(2)}, u32[]{:S(2)}) collective-permute-start(bf16[4,128,256]{2,1,0:T(8,128)(2,1)S(1)} %get-tuple-element.198.refs_4_), channel_id=1, source_target_pairs={{0,1},{1,0},{2,3},{3,2},{4,5},{5,4},{6,7},{7,6},{8,9},{9,8},{10,11... | collective-permute-start | bytes 786440 | tf_op jit(solution)/shard_map/ppermute | solution.py:42
  53.6 6.6 %collective-permute-start.31 = (bf16[4,128,256]{2,1,0:T(8,128)(2,1)S(1)}, bf16[4,128,256]{2,1,0:T(8,128)(2,1)S(1)}, u32[]{:S(2)}, u32[]{:S(2)}) collective-permute-start(bf16[4,128,256]{2,1,0:T(8,128)(2,1)S(1)} %collective-permute-done.20.refs_2_), channel_id=1, source_target_pairs={{0,1},{1,0},{2,3},{3,2},{4,5},{5,4},{6,7},{7,6},{8,9},{9,8},{10,11... | collective-permute-start | bytes 786440 | tf_op jit(solution)/shard_map/ppermute | solution.py:42
  54.1 6.2 %collective-permute-start.32 = (bf16[4,128,256]{2,1,0:T(8,128)(2,1)S(1)}, bf16[4,128,256]{2,1,0:T(8,128)(2,1)S(1)}, u32[]{:S(2)}, u32[]{:S(2)}) collective-permute-start(bf16[4,128,256]{2,1,0:T(8,128)(2,1)S(1)} %collective-permute-done.23.refs_6_), channel_id=1, source_target_pairs={{0,1},{1,0},{2,3},{3,2},{4,5},{5,4},{6,7},{7,6},{8,9},{9,8},{10,11... | collective-permute-start | bytes 786440 | tf_op jit(solution)/shard_map/ppermute | solution.py:42
  56.5 8.5 %collective-permute-start.33 = (bf16[4,128,256]{2,1,0:T(8,128)(2,1)S(1)}, bf16[4,128,256]{2,1,0:T(8,128)(2,1)S(1)}, u32[]{:S(2)}, u32[]{:S(2)}) collective-permute-start(bf16[4,128,256]{2,1,0:T(8,128)(2,1)S(1)} %get-tuple-element.198.refs_4_), channel_id=1, source_target_pairs={{0,2},{2,0},{1,3},{3,1},{4,6},{6,4},{5,7},{7,5},{8,10},{10,8},{9,1... | collective-permute-start | bytes 786440 | tf_op jit(solution)/shard_map/ppermute | solution.py:42
  58.2 15.1 %collective-permute-start.25 = (bf16[4,128,256]{2,1,0:T(8,128)(2,1)S(1)}, bf16[4,128,256]{2,1,0:T(8,128)(2,1)S(1)}, u32[]{:S(2)}, u32[]{:S(2)}) collective-permute-start(bf16[4,128,256]{2,1,0:T(8,128)(2,1)S(1)} %get-tuple-element.156), channel_id=1, source_target_pairs={{0,4},{4,8},{8,12},{12,0},{1,5},{5,9},{9,13},{13,1},{2,6},{6,10},{... | collective-permute-start | bytes 786440 | tf_op jit(solution)/shard_map/ppermute | solution.py:350
  60.2 13.2 %collective-permute-start.29 = (bf16[4,128,256]{2,1,0:T(8,128)(2,1)S(1)}, bf16[4,128,256]{2,1,0:T(8,128)(2,1)S(1)}, u32[]{:S(2)}, u32[]{:S(2)}) collective-permute-start(bf16[4,128,256]{2,1,0:T(8,128)(2,1)S(1)} %get-tuple-element.165), channel_id=1, source_target_pairs={{0,4},{4,8},{8,12},{12,0},{1,5},{5,9},{9,13},{13,1},{2,6},{6,10},{... | collective-permute-start | bytes 786440 | tf_op jit(solution)/shard_map/ppermute | solution.py:350
  60.2 13.1 %collective-permute-start.30 = (bf16[4,128,256]{2,1,0:T(8,128)(2,1)S(1)}, bf16[4,128,256]{2,1,0:T(8,128)(2,1)S(1)}, u32[]{:S(2)}, u32[]{:S(2)}) collective-permute-start(bf16[4,128,256]{2,1,0:T(8,128)(2,1)S(1)} %get-tuple-element.202.refs_8_), channel_id=1, source_target_pairs={{0,1},{1,0},{2,3},{3,2},{4,5},{5,4},{6,7},{7,6},{8,9},{9,8},{10,11... | collective-permute-start | bytes 786440 | tf_op jit(solution)/shard_map/ppermute | solution.py:42
  60.3 18.3 %collective-permute-start.38 = (bf16[4,128,256]{2,1,0:T(8,128)(2,1)S(1)}, bf16[4,128,256]{2,1,0:T(8,128)(2,1)S(1)}, u32[]{:S(2)}, u32[]{:S(2)}) collective-permute-start(bf16[4,128,256]{2,1,0:T(8,128)(2,1)S(1)} %get-tuple-element.202.refs_8_), channel_id=1, source_target_pairs={{0,2},{2,0},{1,3},{3,1},{4,6},{6,4},{5,7},{7,5},{8,10},{10,8},{9,1... | collective-permute-start | bytes 786440 | tf_op jit(solution)/shard_map/ppermute | solution.py:42
  75.5 12.6 %collective-permute-start.35 = (bf16[8,128,256]{2,1,0:T(8,128)(2,1)S(1)}, bf16[8,128,256]{2,1,0:T(8,128)(2,1)S(1)}, u32[]{:S(2)}, u32[]{:S(2)}) collective-permute-start(bf16[8,128,256]{2,1,0:T(8,128)(2,1)S(1)} %pack.11.refs_0_), channel_id=1, source_target_pairs={{0,2},{2,0},{1,3},{3,1},{4,6},{6,4},{5,7},{7,5},{8,10},{10,8},{9,1... | collective-permute-start | bytes 1572872 | tf_op jit(solution)/shard_map/ppermute | solution.py:42
  78.1 10.1 %collective-permute-start.34 = (bf16[8,128,256]{2,1,0:T(8,128)(2,1)S(1)}, bf16[8,128,256]{2,1,0:T(8,128)(2,1)S(1)}, u32[]{:S(2)}, u32[]{:S(2)}) collective-permute-start(bf16[8,128,256]{2,1,0:T(8,128)(2,1)S(1)} %pack.11.refs_0_), channel_id=1, source_target_pairs={{0,1},{1,0},{2,3},{3,2},{4,5},{5,4},{6,7},{7,6},{8,9},{9,8},{10,11... | collective-permute-start | bytes 1572872 | tf_op jit(solution)/shard_map/ppermute | solution.py:42
  (13 other events, 109.7 us)

commit v3 on v2

--- a/solution.py
+++ b/solution.py
@@ -427,8 +427,8 @@
         if number + 1 < SWEEPS:
             across = [parts[2] for parts in pieces[:number]] if number + 2 < SWEEPS else []
             came = slice(number + 1, number + 2 if number + 2 < SWEEPS else None)
-            flights[came], across, pieces[number][1], gain, slots, marks, held = lax.optimization_barrier(
-                (flights[came], across, pieces[number][1], gain, slots, marks, held)
+            flights[came], across, pieces[number][1], gain, slots, marks, counts, held = lax.optimization_barrier(
+                (flights[came], across, pieces[number][1], gain, slots, marks, counts, held)
             )
             for parts, arrived in zip(pieces, across):
                 parts[2] = arrived

time: 109 us -> 107 us (0.982)
  Pallas kernels: 47.9 us -> 45.4 us
    pallas_call x3, Pallas kernels: 23.7 us -> 20.6 us  [project(): pl.pallas_call(kernel, out_shape=(out, out), grid_spec=pltpu.PrefetchScal...]
  transfers between devices with their start and end apart: 32 -> 32, of which waited for: 12 -> 12; matrix products, arithmetic and copies ran while one was open for 6% -> 6% of each run, Pallas kernels for 27% -> 28%
where the time goes in v3:
time: 107 us; the launch traced here: 106 us
  Pallas kernels  45.4 us (42%)
  waiting for transfers between devices  29.9 us (28%)
  starting transfers between devices  20.4 us (19%)
  local copies, waits for them, and re-layouts  7.11 us (7%)
  other arithmetic  2.66 us (2%)
    pallas_call x3, Pallas kernels, project(): pl.pallas_call(kernel, out_shape=(out, out), grid_spec=pltpu.PrefetchScal...  20.6 us
    ppermute x7, waiting for transfers between devices, onward(): lax.ppermute(value, 'seq', [(chip, (chip + 1) % size) for chip in range(s...  19.9 us
    ppermute x22, starting transfers between devices, swapped(): return lax.ppermute(value, axis, [(0, 1), (1, 0)])  12.5 us
    pallas_call x6, Pallas kernels, pack(): pl.pallas_call(kernel, out_shape=tuple((jax.ShapeDtypeStruct((cap,) + poo...  12 us
    pallas_call x1, Pallas kernels, attend(): pl.pallas_call(attend_kernel, out_shape=jax.ShapeDtypeStruct(queries.shap...  10.2 us
    ppermute x22, waiting for transfers between devices, swapped(): return lax.ppermute(value, axis, [(0, 1), (1, 0)])  9.13 us
    ppermute x3, starting transfers between devices, exchanged_table(): lax.ppermute(codes, 'seq', [(chip, chip ^ offset) for chip in range(CHIPS)])  5.76 us
    pallas_call x1, Pallas kernels, make_plan(): pl.pallas_call(plan_kernel, out_shape=jax.ShapeDtypeStruct((8, LANES), jn...  2.53 us
  transfers between devices with their start and end apart: 32, of which 12 were waited for; matrix products, arithmetic and copies ran while one was open for 6% of the time, Pallas kernels for 28%

profile of v3, /device:TPU:0, one launch (start us, length us, event | category | flops | bytes accessed | tf_op | source)
XLA Modules:
  0.0 106.5 jit_solution(16737572702289753325)
XLA Ops:
  0.9 1.3 %fusion.7 = (bf16[8,128,256]{2,1,0:T(8,128)(2,1)S(1)}, bf16[8,128,256]{2,1,0:T(8,128)(2,1)S(1)}) fusion(bf16[16,128,256]{2,1,0:T(8,128)(2,1)} %refs_0_.11), kind=kLoop, calls=%fused_computation.38 | loop fusion | bytes 2097152 | tf_op jit(solution)/shard_map/slice | solution.py:394
  2.2 5.1 %collective-permute-start.11 = (s32[24]{0:T(128)S(1)}, s32[24]{0:T(128)S(1)}, u32[]{:S(2)}, u32[]{:S(2)}) collective-permute-start(s32[24]{0:T(128)S(1)} %reshape.130), channel_id=1, source_target_pairs={{0,12},{4,8},{8,4},{12,0},{1,13},{5,9},{9,5},{13,1},{2,14},{6,10},... | collective-permute-start | bytes 296 | tf_op jit(solution)/shard_map/ppermute | solution.py:382
  7.9 1.6 %collective-permute-start.17 = (f32[1,256]{1,0:T(1,128)}, f32[1,256]{1,0:T(1,128)S(1)}, u32[]{:S(2)}, u32[]{:S(2)}) collective-permute-start(f32[1,256]{1,0:T(1,128)} %bitcast.39), channel_id=1, source_target_pairs={{0,2},{2,0},{1,3},{3,1},{4,6},{6,4},{5,7},{7,5},{8,10},{10,8},{9,1... | collective-permute-start | bytes 3080 | tf_op jit(solution)/shard_map/ppermute | solution.py:42
  11.7 1.6 %collective-permute-start.12 = (s32[4,24]{1,0:T(4,128)S(1)}, s32[4,24]{1,0:T(4,128)S(1)}, u32[]{:S(2)}, u32[]{:S(2)}) collective-permute-start(s32[4,24]{1,0:T(4,128)S(1)} %pad_add_fusion.2), channel_id=1, source_target_pairs={{0,16},{16,0},{1,17},{17,1},{2,18},{18,2},{3,19},{19,3},{4,20},{20... | collective-permute-start | bytes 1160 | tf_op jit(solution)/shard_map/ppermute | solution.py:42
  13.9 1.5 %collective-permute-done.12 = s32[4,24]{1,0:T(4,128)S(1)} collective-permute-done((s32[4,24]{1,0:T(4,128)S(1)}, s32[4,24]{1,0:T(4,128)S(1)}, u32[]{:S(2)}, u32[]{:S(2)}) %collective-permute-start.12) | collective-permute-done | bytes 416 | tf_op jit(solution)/shard_map/ppermute | solution.py:42
  16.5 2.5 %plan.1 = s32[8,128]{1,0:T(8,128)} custom-call(s32[1]{0:T(128)} %bitcast.2.place, s32[192]{0:T(256)} %reshape.131.table), custom_call_target="tpu_custom_call" | custom-call | tf_op jit(solution)/shard_map/plan/pallas_call | solution.py:286
  21.4 4.7 %collective-permute-done.13.refs_1_ = bf16[8,128,256]{2,1,0:T(8,128)(2,1)S(1)} collective-permute-done((bf16[8,128,256]{2,1,0:T(8,128)(2,1)S(1)}, bf16[8,128,256]{2,1,0:T(8,128)(2,1)S(1)}, u32[]{:S(2)}, u32[]{:S(2)}) %collective-permute-start.13) | collective-permute-done | bytes 524320 | tf_op jit(solution)/shard_map/ppermute | solution.py:350
  26.8 1.9 %pack.6 = (bf16[4,128,256]{2,1,0:T(8,128)(2,1)S(1)}, bf16[4,128,256]{2,1,0:T(8,128)(2,1)S(1)}) custom-call(s32[1024]{0:T(1024)S(1)} %bitcast.23, bf16[16,128,256]{2,1,0:T(8,128)(2,1)} %refs_0_.11, bf16[8,128,256]{2,1,0:T(8,128)(2,1)S(1)} %collective-permute-done.13.refs_1_), custom_call_target="tpu_custom_call" | custom-call | flops 1 | bytes 1 | tf_op jit(solution)/shard_map/pack/pallas_call | solution.py:314
  32.4 4.9 %collective-permute-done.14.refs_2_ = bf16[8,128,256]{2,1,0:T(8,128)(2,1)S(1)} collective-permute-done((bf16[8,128,256]{2,1,0:T(8,128)(2,1)S(1)}, bf16[8,128,256]{2,1,0:T(8,128)(2,1)S(1)}, u32[]{:S(2)}, u32[]{:S(2)}) %collective-permute-start.14) | collective-permute-done | bytes 524320 | tf_op jit(solution)/shard_map/ppermute | solution.py:350
  38.0 2.3 %pack.7 = (bf16[4,128,256]{2,1,0:T(8,128)(2,1)S(1)}, bf16[4,128,256]{2,1,0:T(8,128)(2,1)S(1)}) custom-call(s32[1024]{0:T(1024)S(1)} %bitcast.24, bf16[16,128,256]{2,1,0:T(8,128)(2,1)} %refs_0_.11, bf16[8,128,256]{2,1,0:T(8,128)(2,1)S(1)} %collective-permute-done.13.refs_1_, bf16[8,128,256]{2,1,0:T(8,128)(2,1)S(1)} %collective-permute-done.14.refs_2_), custom_call_target="tpu_custom_call" | custom-call | flops 1 | bytes 1 | tf_op jit(solution)/shard_map/pack/pallas_call | solution.py:314
  40.6 2.0 %collective-permute-done.19.refs_3_ = bf16[4,128,256]{2,1,0:T(8,128)(2,1)S(1)} collective-permute-done((bf16[4,128,256]{2,1,0:T(8,128)(2,1)S(1)}, bf16[4,128,256]{2,1,0:T(8,128)(2,1)S(1)}, u32[]{:S(2)}, u32[]{:S(2)}) %collective-permute-start.19) | collective-permute-done | bytes 262176 | tf_op jit(solution)/shard_map/ppermute | solution.py:350
  42.6 1.9 %pack.8 = (bf16[4,128,256]{2,1,0:T(8,128)(2,1)S(1)}, bf16[4,128,256]{2,1,0:T(8,128)(2,1)S(1)}) custom-call(s32[1024]{0:T(1024)S(1)} %bitcast.25, bf16[16,128,256]{2,1,0:T(8,128)(2,1)} %refs_0_.11, bf16[8,128,256]{2,1,0:T(8,128)(2,1)S(1)} %collective-permute-done.13.refs_1_, bf16[8,128,256]{2,1,0:T(8,128)(2,1)S(1)} %collective-permute-done.14.refs_2_, ...), custom_call_target="tpu_custom_call" | custom-call | flops 1 | bytes 1 | tf_op jit(solution)/shard_map/pack/pallas_call | solution.py:314
  45.5 6.1 %collective-permute-done.22.refs_4_ = bf16[4,128,256]{2,1,0:T(8,128)(2,1)S(1)} collective-permute-done((bf16[4,128,256]{2,1,0:T(8,128)(2,1)S(1)}, bf16[4,128,256]{2,1,0:T(8,128)(2,1)S(1)}, u32[]{:S(2)}, u32[]{:S(2)}) %collective-permute-start.22) | collective-permute-done | bytes 262176 | tf_op jit(solution)/shard_map/ppermute | solution.py:350
  51.6 1.9 %pack.9 = (bf16[4,128,256]{2,1,0:T(8,128)(2,1)S(1)}, bf16[4,128,256]{2,1,0:T(8,128)(2,1)S(1)}) custom-call(s32[1024]{0:T(1024)S(1)} %bitcast.26, bf16[16,128,256]{2,1,0:T(8,128)(2,1)} %refs_0_.11, bf16[8,128,256]{2,1,0:T(8,128)(2,1)S(1)} %collective-permute-done.13.refs_1_, bf16[8,128,256]{2,1,0:T(8,128)(2,1)S(1)} %collective-permute-done.14.refs_2_, ...), custom_call_target="tpu_custom_call" | custom-call | flops 1 | bytes 1 | tf_op jit(solution)/shard_map/pack/pallas_call | solution.py:314
  54.2 2.3 %collective-permute-done.26.refs_5_ = bf16[4,128,256]{2,1,0:T(8,128)(2,1)S(1)} collective-permute-done((bf16[4,128,256]{2,1,0:T(8,128)(2,1)S(1)}, bf16[4,128,256]{2,1,0:T(8,128)(2,1)S(1)}, u32[]{:S(2)}, u32[]{:S(2)}) %collective-permute-start.26) | collective-permute-done | bytes 262176 | tf_op jit(solution)/shard_map/ppermute | solution.py:350
  56.5 1.8 %collective-permute-start.33 = (bf16[4,128,256]{2,1,0:T(8,128)(2,1)S(1)}, bf16[4,128,256]{2,1,0:T(8,128)(2,1)S(1)}, u32[]{:S(2)}, u32[]{:S(2)}) collective-permute-start(bf16[4,128,256]{2,1,0:T(8,128)(2,1)S(1)} %get-tuple-element.207.refs_4_), channel_id=1, source_target_pairs={{0,2},{2,0},{1,3},{3,1},{4,6},{6,4},{5,7},{7,5},{8,10},{10,8},{9,1... | collective-permute-start | bytes 786440 | tf_op jit(solution)/shard_map/ppermute | solution.py:42
  58.3 1.8 %pack.10 = (bf16[4,128,256]{2,1,0:T(8,128)(2,1)S(1)}, bf16[4,128,256]{2,1,0:T(8,128)(2,1)S(1)}) custom-call(s32[1024]{0:T(1024)S(1)} %bitcast.27, bf16[16,128,256]{2,1,0:T(8,128)(2,1)} %refs_0_.11, bf16[8,128,256]{2,1,0:T(8,128)(2,1)S(1)} %collective-permute-done.13.refs_1_, bf16[8,128,256]{2,1,0:T(8,128)(2,1)S(1)} %collective-permute-done.14.refs_2_, ...), custom_call_target="tpu_custom_call" | custom-call | flops 1 | bytes 1 | tf_op jit(solution)/shard_map/pack/pallas_call | solution.py:314
  60.5 4.5 %collective-permute-done.33.refs_6_ = bf16[4,128,256]{2,1,0:T(8,128)(2,1)S(1)} collective-permute-done((bf16[4,128,256]{2,1,0:T(8,128)(2,1)S(1)}, bf16[4,128,256]{2,1,0:T(8,128)(2,1)S(1)}, u32[]{:S(2)}, u32[]{:S(2)}) %collective-permute-start.33) | collective-permute-done | bytes 262176 | tf_op jit(solution)/shard_map/ppermute | solution.py:42
  65.0 8.3 %project.5 = (bf16[176,128,1024]{2,1,0:T(8,128)(2,1)}, bf16[176,128,1024]{2,1,0:T(8,128)(2,1)}) custom-call(s32[32]{0:T(128)S(1)} %concatenate.23.marks_ref, f32[1,1024]{1,0:T(1,128)S(1)} %pad_maximum_fusion.gain_ref, bf16[4,128,256]{2,1,0:T(8,128)(2,1)S(1)} %get-tuple-element.183.refs_0_, bf16[4,128,256]{2,1,0:T(8,128)(2,1)S(1)} %collective-permute-done.15.refs_1_, ...), custom_call_target="tpu_custom_call" | custom-call | flops 1 | bytes 1 | tf_op jit(solution)/shard_map/project/pallas_call | solution.py:103
  73.4 2.1 %pack.11.refs_0_ = bf16[8,128,256]{2,1,0:T(8,128)(2,1)S(1)} custom-call(s32[1024]{0:T(1024)S(1)} %bitcast.28, bf16[16,128,256]{2,1,0:T(8,128)(2,1)} %refs_0_.11, bf16[8,128,256]{2,1,0:T(8,128)(2,1)S(1)} %collective-permute-done.13.refs_1_, bf16[8,128,256]{2,1,0:T(8,128)(2,1)S(1)} %collective-permute-done.14.refs_2_, ...), custom_call_target="tpu_custom_call" | custom-call | flops 1 | bytes 1 | tf_op jit(solution)/shard_map/pack/pallas_call | solution.py:314
  75.5 2.6 %collective-permute-start.35 = (bf16[8,128,256]{2,1,0:T(8,128)(2,1)S(1)}, bf16[8,128,256]{2,1,0:T(8,128)(2,1)S(1)}, u32[]{:S(2)}, u32[]{:S(2)}) collective-permute-start(bf16[8,128,256]{2,1,0:T(8,128)(2,1)S(1)} %pack.11.refs_0_), channel_id=1, source_target_pairs={{0,2},{2,0},{1,3},{3,1},{4,6},{6,4},{5,7},{7,5},{8,10},{10,8},{9,1... | collective-permute-start | bytes 1572872 | tf_op jit(solution)/shard_map/ppermute | solution.py:42
  81.1 7.0 %project.6 = (bf16[176,128,1024]{2,1,0:T(8,128)(2,1)}, bf16[176,128,1024]{2,1,0:T(8,128)(2,1)}) custom-call(s32[32]{0:T(128)S(1)} %concatenate.23.marks_ref, f32[1,1024]{1,0:T(1,128)S(1)} %pad_maximum_fusion.gain_ref, bf16[4,128,256]{2,1,0:T(8,128)(2,1)S(1)} %get-tuple-element.203.refs_0_, ...), custom_call_target="tpu_custom_call", output_to_operand_aliasing={{0}: (16, {}), {1}: (17, {})} | custom-call | flops 1 | bytes 1 | tf_op jit(solution)/shard_map/project/pallas_call | solution.py:103
  90.1 5.3 %project.7 = (bf16[176,128,1024]{2,1,0:T(8,128)(2,1)}, bf16[176,128,1024]{2,1,0:T(8,128)(2,1)}) custom-call(s32[32]{0:T(128)S(1)} %concatenate.23.marks_ref, f32[1,1024]{1,0:T(1,128)S(1)} %pad_maximum_fusion.gain_ref, bf16[8,128,256]{2,1,0:T(8,128)(2,1)S(1)} %pack.11.refs_0_, ...), custom_call_target="tpu_custom_call", output_to_operand_aliasing={{0}: (8, {}), {1}: (9, {})} | custom-call | flops 1 | bytes 1 | tf_op jit(solution)/shard_map/project/pallas_call | solution.py:103
  96.3 10.2 %attend.1 = bf16[768,1024]{1,0:T(8,128)(2,1)} custom-call(s32[24]{0:T(128)} %get-tuple-element.226.slots, s32[12]{0:T(128)} %convert_reduce_fusion.counts, bf16[768,1024]{1,0:T(8,128)(2,1)} %query_ref.1, bf16[176,128,1024]{2,1,0:T(8,128)(2,1)} %get-tuple-element.228.refs_0_.refs_1_.refs_2_.refs_3_.refs_4_.refs_5_, ...), custom_call_target="tpu_custom_call" | custom-call | flops 1 | bytes 1 | tf_op jit(solution)/shard_map/attend/pallas_call | solution.py:179
  (90 shorter events, 21.1 us)
Async XLA Ops:
  2.2 7.4 %collective-permute-start.11 = (s32[24]{0:T(128)S(1)}, s32[24]{0:T(128)S(1)}, u32[]{:S(2)}, u32[]{:S(2)}) collective-permute-start(s32[24]{0:T(128)S(1)} %reshape.130), channel_id=1, source_target_pairs={{0,12},{4,8},{8,4},{12,0},{1,13},{5,9},{9,5},{13,1},{2,14},{6,10},... | collective-permute-start | bytes 296 | tf_op jit(solution)/shard_map/ppermute | solution.py:382
  7.3 4.4 %collective-permute-start.10 = (s32[24]{0:T(128)S(1)}, s32[24]{0:T(128)S(1)}, u32[]{:S(2)}, u32[]{:S(2)}) collective-permute-start(s32[24]{0:T(128)S(1)} %reshape.130), channel_id=1, source_target_pairs={{0,8},{4,12},{8,0},{12,4},{1,9},{5,13},{9,1},{13,5},{2,10},{6,14},... | collective-permute-start | bytes 296 | tf_op jit(solution)/shard_map/ppermute | solution.py:382
  7.9 21.0 %collective-permute-start.17 = (f32[1,256]{1,0:T(1,128)}, f32[1,256]{1,0:T(1,128)S(1)}, u32[]{:S(2)}, u32[]{:S(2)}) collective-permute-start(f32[1,256]{1,0:T(1,128)} %bitcast.39), channel_id=1, source_target_pairs={{0,2},{2,0},{1,3},{3,1},{4,6},{6,4},{5,7},{7,5},{8,10},{10,8},{9,1... | collective-permute-start | bytes 3080 | tf_op jit(solution)/shard_map/ppermute | solution.py:42
  9.6 21.2 %collective-permute-start.16 = (f32[1,256]{1,0:T(1,128)}, f32[1,256]{1,0:T(1,128)S(1)}, u32[]{:S(2)}, u32[]{:S(2)}) collective-permute-start(f32[1,256]{1,0:T(1,128)} %bitcast.40), channel_id=1, source_target_pairs={{0,1},{1,0},{2,3},{3,2},{4,5},{5,4},{6,7},{7,6},{8,9},{9,8},{10,11... | collective-permute-start | bytes 3080 | tf_op jit(solution)/shard_map/ppermute | solution.py:42
  9.6 16.5 %collective-permute-start.13 = (bf16[8,128,256]{2,1,0:T(8,128)(2,1)S(1)}, bf16[8,128,256]{2,1,0:T(8,128)(2,1)S(1)}, u32[]{:S(2)}, u32[]{:S(2)}) collective-permute-start(bf16[8,128,256]{2,1,0:T(8,128)(2,1)S(1)} %get-tuple-element.143), channel_id=1, source_target_pairs={{0,4},{4,8},{8,12},{12,0},{1,5},{5,9},{9,13},{13,1},{2,6},{6,10},{... | collective-permute-start | bytes 1572872 | tf_op jit(solution)/shard_map/ppermute | solution.py:350
  13.3 24.0 %collective-permute-start.14 = (bf16[8,128,256]{2,1,0:T(8,128)(2,1)S(1)}, bf16[8,128,256]{2,1,0:T(8,128)(2,1)S(1)}, u32[]{:S(2)}, u32[]{:S(2)}) collective-permute-start(bf16[8,128,256]{2,1,0:T(8,128)(2,1)S(1)} %get-tuple-element.144), channel_id=1, source_target_pairs={{0,4},{4,8},{8,12},{12,0},{1,5},{5,9},{9,13},{13,1},{2,6},{6,10},{... | collective-permute-start | bytes 1572872 | tf_op jit(solution)/shard_map/ppermute | solution.py:350
  28.7 8.6 %collective-permute-start.15 = (bf16[4,128,256]{2,1,0:T(8,128)(2,1)S(1)}, bf16[4,128,256]{2,1,0:T(8,128)(2,1)S(1)}, u32[]{:S(2)}, u32[]{:S(2)}) collective-permute-start(bf16[4,128,256]{2,1,0:T(8,128)(2,1)S(1)} %get-tuple-element.183.refs_0_), channel_id=1, source_target_pairs={{0,1},{1,0},{2,3},{3,2},{4,5},{5,4},{6,7},{7,6},{8,9},{9,8},{10,11... | collective-permute-start | bytes 786440 | tf_op jit(solution)/shard_map/ppermute | solution.py:42
  31.4 11.2 %collective-permute-start.20 = (bf16[4,128,256]{2,1,0:T(8,128)(2,1)S(1)}, bf16[4,128,256]{2,1,0:T(8,128)(2,1)S(1)}, u32[]{:S(2)}, u32[]{:S(2)}) collective-permute-start(bf16[4,128,256]{2,1,0:T(8,128)(2,1)S(1)} %get-tuple-element.183.refs_0_), channel_id=1, source_target_pairs={{0,2},{2,0},{1,3},{3,1},{4,6},{6,4},{5,7},{7,5},{8,10},{10,8},{9,1... | collective-permute-start | bytes 786440 | tf_op jit(solution)/shard_map/ppermute | solution.py:42
  32.4 10.2 %collective-permute-start.19 = (bf16[4,128,256]{2,1,0:T(8,128)(2,1)S(1)}, bf16[4,128,256]{2,1,0:T(8,128)(2,1)S(1)}, u32[]{:S(2)}, u32[]{:S(2)}) collective-permute-start(bf16[4,128,256]{2,1,0:T(8,128)(2,1)S(1)} %get-tuple-element.148), channel_id=1, source_target_pairs={{0,4},{4,8},{8,12},{12,0},{1,5},{5,9},{9,13},{13,1},{2,6},{6,10},{... | collective-permute-start | bytes 786440 | tf_op jit(solution)/shard_map/ppermute | solution.py:350
  40.4 11.2 %collective-permute-start.23 = (bf16[4,128,256]{2,1,0:T(8,128)(2,1)S(1)}, bf16[4,128,256]{2,1,0:T(8,128)(2,1)S(1)}, u32[]{:S(2)}, u32[]{:S(2)}) collective-permute-start(bf16[4,128,256]{2,1,0:T(8,128)(2,1)S(1)} %get-tuple-element.187.refs_4_), channel_id=1, source_target_pairs={{0,2},{2,0},{1,3},{3,1},{4,6},{6,4},{5,7},{7,5},{8,10},{10,8},{9,1... | collective-permute-start | bytes 786440 | tf_op jit(solution)/shard_map/ppermute | solution.py:42
  40.6 10.9 %collective-permute-start.22 = (bf16[4,128,256]{2,1,0:T(8,128)(2,1)S(1)}, bf16[4,128,256]{2,1,0:T(8,128)(2,1)S(1)}, u32[]{:S(2)}, u32[]{:S(2)}) collective-permute-start(bf16[4,128,256]{2,1,0:T(8,128)(2,1)S(1)} %get-tuple-element.155), channel_id=1, source_target_pairs={{0,4},{4,8},{8,12},{12,0},{1,5},{5,9},{9,13},{13,1},{2,6},{6,10},{... | collective-permute-start | bytes 786440 | tf_op jit(solution)/shard_map/ppermute | solution.py:350
  44.5 7.1 %collective-permute-start.24 = (bf16[4,128,256]{2,1,0:T(8,128)(2,1)S(1)}, bf16[4,128,256]{2,1,0:T(8,128)(2,1)S(1)}, u32[]{:S(2)}, u32[]{:S(2)}) collective-permute-start(bf16[4,128,256]{2,1,0:T(8,128)(2,1)S(1)} %get-tuple-element.203.refs_0_), channel_id=1, source_target_pairs={{0,1},{1,0},{2,3},{3,2},{4,5},{5,4},{6,7},{7,6},{8,9},{9,8},{10,11... | collective-permute-start | bytes 786440 | tf_op jit(solution)/shard_map/ppermute | solution.py:42
  44.6 13.6 %collective-permute-start.27 = (bf16[4,128,256]{2,1,0:T(8,128)(2,1)S(1)}, bf16[4,128,256]{2,1,0:T(8,128)(2,1)S(1)}, u32[]{:S(2)}, u32[]{:S(2)}) collective-permute-start(bf16[4,128,256]{2,1,0:T(8,128)(2,1)S(1)} %get-tuple-element.203.refs_0_), channel_id=1, source_target_pairs={{0,2},{2,0},{1,3},{3,1},{4,6},{6,4},{5,7},{7,5},{8,10},{10,8},{9,1... | collective-permute-start | bytes 786440 | tf_op jit(solution)/shard_map/ppermute | solution.py:42
  45.3 11.2 %collective-permute-start.26 = (bf16[4,128,256]{2,1,0:T(8,128)(2,1)S(1)}, bf16[4,128,256]{2,1,0:T(8,128)(2,1)S(1)}, u32[]{:S(2)}, u32[]{:S(2)}) collective-permute-start(bf16[4,128,256]{2,1,0:T(8,128)(2,1)S(1)} %get-tuple-element.164), channel_id=1, source_target_pairs={{0,4},{4,8},{8,12},{12,0},{1,5},{5,9},{9,13},{13,1},{2,6},{6,10},{... | collective-permute-start | bytes 786440 | tf_op jit(solution)/shard_map/ppermute | solution.py:350
  53.5 4.7 %collective-permute-start.28 = (bf16[4,128,256]{2,1,0:T(8,128)(2,1)S(1)}, bf16[4,128,256]{2,1,0:T(8,128)(2,1)S(1)}, u32[]{:S(2)}, u32[]{:S(2)}) collective-permute-start(bf16[4,128,256]{2,1,0:T(8,128)(2,1)S(1)} %get-tuple-element.207.refs_4_), channel_id=1, source_target_pairs={{0,1},{1,0},{2,3},{3,2},{4,5},{5,4},{6,7},{7,6},{8,9},{9,8},{10,11... | collective-permute-start | bytes 786440 | tf_op jit(solution)/shard_map/ppermute | solution.py:42
  53.6 6.5 %collective-permute-start.31 = (bf16[4,128,256]{2,1,0:T(8,128)(2,1)S(1)}, bf16[4,128,256]{2,1,0:T(8,128)(2,1)S(1)}, u32[]{:S(2)}, u32[]{:S(2)}) collective-permute-start(bf16[4,128,256]{2,1,0:T(8,128)(2,1)S(1)} %collective-permute-done.20.refs_2_), channel_id=1, source_target_pairs={{0,1},{1,0},{2,3},{3,2},{4,5},{5,4},{6,7},{7,6},{8,9},{9,8},{10,11... | collective-permute-start | bytes 786440 | tf_op jit(solution)/shard_map/ppermute | solution.py:42
  54.1 6.1 %collective-permute-start.32 = (bf16[4,128,256]{2,1,0:T(8,128)(2,1)S(1)}, bf16[4,128,256]{2,1,0:T(8,128)(2,1)S(1)}, u32[]{:S(2)}, u32[]{:S(2)}) collective-permute-start(bf16[4,128,256]{2,1,0:T(8,128)(2,1)S(1)} %collective-permute-done.23.refs_6_), channel_id=1, source_target_pairs={{0,1},{1,0},{2,3},{3,2},{4,5},{5,4},{6,7},{7,6},{8,9},{9,8},{10,11... | collective-permute-start | bytes 786440 | tf_op jit(solution)/shard_map/ppermute | solution.py:42
  56.5 8.5 %collective-permute-start.33 = (bf16[4,128,256]{2,1,0:T(8,128)(2,1)S(1)}, bf16[4,128,256]{2,1,0:T(8,128)(2,1)S(1)}, u32[]{:S(2)}, u32[]{:S(2)}) collective-permute-start(bf16[4,128,256]{2,1,0:T(8,128)(2,1)S(1)} %get-tuple-element.207.refs_4_), channel_id=1, source_target_pairs={{0,2},{2,0},{1,3},{3,1},{4,6},{6,4},{5,7},{7,5},{8,10},{10,8},{9,1... | collective-permute-start | bytes 786440 | tf_op jit(solution)/shard_map/ppermute | solution.py:42
  58.2 15.1 %collective-permute-start.25 = (bf16[4,128,256]{2,1,0:T(8,128)(2,1)S(1)}, bf16[4,128,256]{2,1,0:T(8,128)(2,1)S(1)}, u32[]{:S(2)}, u32[]{:S(2)}) collective-permute-start(bf16[4,128,256]{2,1,0:T(8,128)(2,1)S(1)} %get-tuple-element.163), channel_id=1, source_target_pairs={{0,4},{4,8},{8,12},{12,0},{1,5},{5,9},{9,13},{13,1},{2,6},{6,10},{... | collective-permute-start | bytes 786440 | tf_op jit(solution)/shard_map/ppermute | solution.py:350
  60.1 13.3 %collective-permute-start.29 = (bf16[4,128,256]{2,1,0:T(8,128)(2,1)S(1)}, bf16[4,128,256]{2,1,0:T(8,128)(2,1)S(1)}, u32[]{:S(2)}, u32[]{:S(2)}) collective-permute-start(bf16[4,128,256]{2,1,0:T(8,128)(2,1)S(1)} %get-tuple-element.173), channel_id=1, source_target_pairs={{0,4},{4,8},{8,12},{12,0},{1,5},{5,9},{9,13},{13,1},{2,6},{6,10},{... | collective-permute-start | bytes 786440 | tf_op jit(solution)/shard_map/ppermute | solution.py:350
  60.1 13.3 %collective-permute-start.30 = (bf16[4,128,256]{2,1,0:T(8,128)(2,1)S(1)}, bf16[4,128,256]{2,1,0:T(8,128)(2,1)S(1)}, u32[]{:S(2)}, u32[]{:S(2)}) collective-permute-start(bf16[4,128,256]{2,1,0:T(8,128)(2,1)S(1)} %get-tuple-element.211.refs_8_), channel_id=1, source_target_pairs={{0,1},{1,0},{2,3},{3,2},{4,5},{5,4},{6,7},{7,6},{8,9},{9,8},{10,11... | collective-permute-start | bytes 786440 | tf_op jit(solution)/shard_map/ppermute | solution.py:42
  60.2 18.4 %collective-permute-start.38 = (bf16[4,128,256]{2,1,0:T(8,128)(2,1)S(1)}, bf16[4,128,256]{2,1,0:T(8,128)(2,1)S(1)}, u32[]{:S(2)}, u32[]{:S(2)}) collective-permute-start(bf16[4,128,256]{2,1,0:T(8,128)(2,1)S(1)} %get-tuple-element.211.refs_8_), channel_id=1, source_target_pairs={{0,2},{2,0},{1,3},{3,1},{4,6},{6,4},{5,7},{7,5},{8,10},{10,8},{9,1... | collective-permute-start | bytes 786440 | tf_op jit(solution)/shard_map/ppermute | solution.py:42
  75.5 12.6 %collective-permute-start.35 = (bf16[8,128,256]{2,1,0:T(8,128)(2,1)S(1)}, bf16[8,128,256]{2,1,0:T(8,128)(2,1)S(1)}, u32[]{:S(2)}, u32[]{:S(2)}) collective-permute-start(bf16[8,128,256]{2,1,0:T(8,128)(2,1)S(1)} %pack.11.refs_0_), channel_id=1, source_target_pairs={{0,2},{2,0},{1,3},{3,1},{4,6},{6,4},{5,7},{7,5},{8,10},{10,8},{9,1... | collective-permute-start | bytes 1572872 | tf_op jit(solution)/shard_map/ppermute | solution.py:42
  78.1 10.1 %collective-permute-start.34 = (bf16[8,128,256]{2,1,0:T(8,128)(2,1)S(1)}, bf16[8,128,256]{2,1,0:T(8,128)(2,1)S(1)}, u32[]{:S(2)}, u32[]{:S(2)}) collective-permute-start(bf16[8,128,256]{2,1,0:T(8,128)(2,1)S(1)} %pack.11.refs_0_), channel_id=1, source_target_pairs={{0,1},{1,0},{2,3},{3,2},{4,5},{5,4},{6,7},{7,6},{8,9},{9,8},{10,11... | collective-permute-start | bytes 1572872 | tf_op jit(solution)/shard_map/ppermute | solution.py:42
  (13 other events, 109.7 us)
